TPU v7x, 32 devices: a whole 2x2x4 slice. The times are simulated.
32 devices in a mesh: groups: 2 (over x), frames: 16 (over z, y, core).
Axes of the slice: x: 2, y: 2, z: 4, core: 2. Of those that a mesh axis runs over, the one named last changes fastest.
Arguments:
- features: bfloat16 [4096, 1024], P(('groups', 'frames')), parts along dimension 0, may hold values from -6 to 6
- valid_length: int32 [2], P('groups'), parts along dimension 0, may hold values from 1024 to 2048
- ln1_gain: float32 [1024], replicated, may hold values from 0.5 to 1.5
- w_qkv: bfloat16 [1024, 1536], P('frames'), may hold values from -3 to 3
- w_out: bfloat16 [512, 1024], P('frames'), may hold values from -0.25 to 0.25
- ln2_gain: float32 [1024], replicated, may hold values from 0.5 to 1.5
- w_pw1: bfloat16 [1024, 2048], P('frames'), may hold values from -0.1875 to 0.1875
- w_dw: float32 [9, 1024], replicated, may hold values from -2 to 2
- bn_scale: float32 [1024], replicated, may hold values from 0.5 to 2
- bn_shift: float32 [1024], replicated, may hold values from -3 to 3
- w_pw2: bfloat16 [1024, 1024], P('frames'), may hold values from -0.1875 to 0.1875
Outputs:
- block_out: bfloat16 [4096, 1024], P(('groups', 'frames')), parts along dimension 0
There are 2 independent parts, one for each index of `groups`. A program takes and returns all parts, laid end to end along the dimension named above; an argument that names none is the same for every part. Nothing has to cross between parts.
All inputs are finite; a program needn't handle non-finite values.
Results may differ from a plain program's by a relative error of at most 0.0098.
Values may be sent and summed in bfloat16 or wider, within the bound.
A program may use at most 128 MiB of HBM per device.

v0:
```python
import math

import jax
import jax.numpy as jnp
from jax import lax
from jax.sharding import PartitionSpec as P

HEADS = 4
HD = 128


EPSILON = 1e-05


def extended(cells, sides, width):
    for axis, dim in sides:
        count = lax.axis_size(axis)
        ends = count - 1
        head = lax.slice_in_dim(cells, 0, width, axis=dim)
        tail = lax.slice_in_dim(cells, cells.shape[dim] - width, cells.shape[dim], axis=dim)
        cells = jnp.concatenate(
            [
                lax.ppermute(tail, axis, [(i, (i + 1) % count) for i in range(ends)]),
                cells,
                lax.ppermute(head, axis, [((i + 1) % count, i) for i in range(ends)]),
            ],
            axis=dim,
        )
    return cells


def layer_norm(values, gain):
    values = values.astype(jnp.float32)
    mean = jnp.mean(values, axis=-1, keepdims=True)
    centred = values - mean
    variance = jnp.mean(centred * centred, axis=-1, keepdims=True)
    return (centred * lax.rsqrt(variance + EPSILON) * gain).astype(jnp.bfloat16)


def per_device(
    features, valid_length, ln1_gain, w_qkv, w_out, ln2_gain, w_pw1, w_dw, bn_scale, bn_shift, w_pw2
):
    limit = valid_length[0]
    local_rows = features.shape[0]
    width = features.shape[1]
    att_width = w_qkv.shape[1] // 3
    scale = 1.0 / math.sqrt(HD)
    tails = (
        lax.all_gather(w_out, "frames", axis=0, tiled=True),
        lax.all_gather(w_pw1, "frames", axis=0, tiled=True),
        lax.all_gather(w_pw2, "frames", axis=0, tiled=True),
    )
    full_out, full_pw1, full_pw2 = tails
    normed1 = layer_norm(features, ln1_gain)
    qkv = jnp.dot(
        normed1,
        lax.all_gather(w_qkv, "frames", axis=0, tiled=True),
        preferred_element_type=jnp.float32,
    ).astype(jnp.bfloat16)
    query_heads = qkv[:, :att_width].reshape(local_rows, HEADS, HD)
    keys = qkv[:, att_width : 2 * att_width]
    values = qkv[:, 2 * att_width :]
    maxima = jnp.full((HEADS, local_rows), -1e30, jnp.float32)
    key_rows = lax.all_gather(keys, "frames", axis=0, tiled=True)
    value_rows = lax.all_gather(values, "frames", axis=0, tiled=True)
    count = key_rows.shape[0]
    key_heads = key_rows.reshape(count, HEADS, HD)
    value_heads = value_rows.reshape(count, HEADS, HD)
    scores = (
        jnp.einsum("qhd,khd->hqk", query_heads, key_heads, preferred_element_type=jnp.float32)
        * scale
    )
    position = jnp.arange(count, dtype=jnp.int32)
    valid = (position < limit)[None, None, :]
    scores = jnp.where(valid, scores, -1e30)
    fresh = jnp.maximum(maxima, jnp.max(scores, axis=-1))
    weights = jnp.where(valid, jnp.exp(scores - fresh[..., None]), 0.0)
    totals = jnp.sum(weights, axis=-1)
    update = jnp.einsum(
        "hqk,khd->hqd",
        weights.astype(jnp.bfloat16),
        value_heads,
        preferred_element_type=jnp.float32,
    )
    summed = update
    maxima, totals, summed = (fresh, totals, summed)
    context = (
        (summed / totals[..., None])
        .transpose(1, 0, 2)
        .reshape(local_rows, att_width)
        .astype(jnp.bfloat16)
    )
    attended = features.astype(jnp.float32) + jnp.dot(
        context, full_out, preferred_element_type=jnp.float32
    )
    normed2 = layer_norm(attended, ln2_gain)
    both = jnp.dot(normed2, full_pw1, preferred_element_type=jnp.float32)
    frame_index = lax.axis_index("frames") * local_rows + jnp.arange(local_rows, dtype=jnp.int32)
    frame_valid = (frame_index < limit)[:, None]
    gated = jnp.where(frame_valid, both[:, :width] * jax.nn.sigmoid(both[:, width:]), 0.0).astype(
        jnp.bfloat16
    )
    half_window = (w_dw.shape[0] - 1) // 2
    widened = extended(gated, (("frames", 0),), half_window)
    widened = widened.astype(jnp.float32)
    conv = jnp.zeros((local_rows, width), jnp.float32)
    for tap in range(w_dw.shape[0]):
        conv = conv + w_dw[tap][None, :] * widened[tap : tap + local_rows]
    activated = jax.nn.silu(bn_scale * conv + bn_shift).astype(jnp.bfloat16)
    result = attended + jnp.dot(activated, full_pw2, preferred_element_type=jnp.float32)
    return result.astype(jnp.bfloat16)


def solution(mesh):
    placed = (
        P(("groups", "frames"), None),
        P("groups"),
        P(),
        P("frames", None),
        P("frames", None),
        P(),
        P("frames", None),
        P(),
        P(),
        P(),
        P("frames", None),
    )
    return jax.shard_map(
        per_device,
        mesh=mesh,
        in_specs=placed,
        out_specs=P(("groups", "frames"), None),
        check_vma=False,
    )
```

profile of v0, /device:TPU:0, one launch (start us, length us, event | category | flops | bytes accessed | tf_op | source)
XLA Modules:
  0.0 286.1 jit_solution(17644636704648669902)
XLA Ops:
  6.5 0.0 all-gather.7.cloned.1.call-start
  6.5 0.7 all-gather.7.cloned.1.call-update
  7.3 0.0 all-gather.11.cloned.1.call-start
  7.3 1.1 convert_reduce_fusion
  8.4 1.2 fusion.21
  9.6 48.0 %all-gather.7.cloned.1.call-done = bf16[1024,1536]{1,0:T(8,128)(2,1)} async-done(((bf16[64,1536]{1,0:T(8,128)(2,1)}), bf16[1024,1536]{1,0:T(8,128)(2,1)}) %all-gather.7.cloned.1.call-update) | async-done | bytes 3145744 | tf_op jit(solution)/shard_map/all_gather | solution.py:57
  57.6 2.6 convolution_convert_fusion
  60.2 0.7 slice_bitcast_fusion
  60.9 0.0 all-gather.11.cloned.1.call-update
  61.0 0.0 all-gather.9.cloned.1.call-start
  61.0 0.7 all-gather.9.cloned.1.call-update
  61.7 0.0 all-gather.13.cloned.1.call-start
  61.7 0.5 all-gather.13.cloned.1.call-update
  62.3 0.0 all-gather.15.cloned.1.call-start
  62.3 0.5 all-gather.15.cloned.1.call-update
  62.9 0.0 all-gather.17.cloned.1.call-start
  62.9 0.5 all-gather.17.cloned.1.call-update
  64.1 37.2 %all-gather.11.cloned.1.call-done = bf16[2048,512]{1,0:T(8,128)(2,1)} async-done(((bf16[128,512]{1,0:T(8,128)(2,1)}), bf16[2048,512]{1,0:T(8,128)(2,1)}) %all-gather.11.cloned.1.call-update) | async-done | bytes 2097168 | tf_op jit(solution)/shard_map/all_gather | solution.py:65
  101.3 2.9 %copy.15 = bf16[2048,512]{0,1:T(8,128)(2,1)S(1)} copy(bf16[2048,512]{1,0:T(8,128)(2,1)} %all-gather.11.cloned.1.call-done) | data formatting | bytes 4194304 | tf_op jit(solution)/shard_map/reshape | solution.py:68
  104.3 39.4 %all-gather.9.cloned.1.call-done = bf16[2048,512]{1,0:T(8,128)(2,1)} async-done(((bf16[128,512]{1,0:T(8,128)(2,1)}), bf16[2048,512]{1,0:T(8,128)(2,1)}) %all-gather.9.cloned.1.call-update) | async-done | bytes 2097168 | tf_op jit(solution)/shard_map/all_gather | solution.py:64
  143.7 2.5 fusion
  146.2 1.1 fusion.1
  147.3 0.0 copy-start
  147.3 0.0 copy-start.2
  147.3 1.3 fusion.16
  148.6 33.8 %all-gather.13.cloned.1.call-done = bf16[512,1024]{1,0:T(8,128)(2,1)} async-done(((bf16[32,1024]{1,0:T(8,128)(2,1)}), bf16[512,1024]{1,0:T(8,128)(2,1)}) %all-gather.13.cloned.1.call-update) | async-done | bytes 1048592 | tf_op jit(solution)/shard_map/all_gather | solution.py:49
  182.5 0.0 copy-done
  182.5 1.6 fusion.68
  184.1 0.0 copy-start.1
  184.1 0.0 copy-start.3
  184.1 0.0 copy-start.4
  184.1 0.2 multiply_reduce_fusion
  184.4 49.6 %all-gather.15.cloned.1.call-done = bf16[1024,2048]{1,0:T(8,128)(2,1)} async-done(((bf16[64,2048]{1,0:T(8,128)(2,1)}), bf16[1024,2048]{1,0:T(8,128)(2,1)}) %all-gather.15.cloned.1.call-update) | async-done | bytes 4194320 | tf_op jit(solution)/shard_map/all_gather | solution.py:50
  234.0 0.0 copy-done.2
  234.0 3.0 %fusion.40 = f32[128,2048]{1,0:T(8,128)S(1)} fusion(bf16[1024,2048]{1,0:T(8,128)(2,1)} %all-gather.15.cloned.1.call-done, f32[128,1024]{1,0:T(8,128)S(1)} %get-tuple-element.22, f32[1024]{0:T(1024)S(1)} %copy-done.2, f32[128]{0:T(128)S(1)} %add_rsqrt_fusion, f32[128]{0:T(128)S(1)} %broadcast_multiply_fusion), kind=kOutput, calls=%fused_computation.54 | convolution fusion | flops 537395200 | bytes 5772288 | tf_op jit(solution)/shard_map/dot_general | solution.py:97
  236.9 0.2 fusion.39
  237.1 2.2 collective-permute-start
  239.3 1.3 collective-permute-start.1
  240.6 0.0 copy-done.1
  240.6 0.0 collective-permute-done
  240.7 1.7 collective-permute-done.1
  242.4 0.1 maximum_convert_fusion
  242.4 33.5 %all-gather.17.cloned.1.call-done = bf16[1024,1024]{1,0:T(8,128)(2,1)} async-done(((bf16[64,1024]{1,0:T(8,128)(2,1)}), bf16[1024,1024]{1,0:T(8,128)(2,1)}) %all-gather.17.cloned.1.call-update) | async-done | bytes 2097168 | tf_op jit(solution)/shard_map/all_gather | solution.py:51
  275.9 0.0 copy-done.3
  275.9 0.0 copy-done.4
  275.9 3.3 %fusion.9 = bf16[128,1024]{1,0:T(8,128)(2,1)} fusion(f32[128,1024]{1,0:T(8,128)S(1)} %get-tuple-element.22, bf16[1024,1024]{1,0:T(8,128)(2,1)} %all-gather.17.cloned.1.call-done, f32[136,1024]{1,0:T(8,128)S(1)} %maximum_convert_fusion, f32[1024]{0:T(1024)S(1)} %copy-done.3, f32[1024]{0:T(1024)S(1)} %bitcast.52, f32[1024]{0:T(1024)S(1)} %bitcast.53, ...), kind=kOutput, calls=%fused_computation.13 | convolution fusion | flops 271843328 | bytes 7647232 | tf_op jit(solution)/shard_map/dot_general | solution.py:110
  (9 shorter events, 0.1 us)
Async XLA Ops:
  6.5 51.0 %all-gather.7.cloned.1.call-start = ((), (), s32[]{:S(2)}) async-start(), calls=%async_computation | async-start | bytes 3342336 | tf_op jit(solution)/shard_map/all_gather | solution.py:57
  7.3 94.1 %all-gather.11.cloned.1.call-start = ((), (), s32[]{:S(2)}) async-start(), calls=%async_computation.2 | async-start | bytes 2228224 | tf_op jit(solution)/shard_map/all_gather | solution.py:65
  61.0 82.7 %all-gather.9.cloned.1.call-start = ((), (), s32[]{:S(2)}) async-start(), calls=%async_computation.1 | async-start | bytes 2228224 | tf_op jit(solution)/shard_map/all_gather | solution.py:64
  61.7 120.8 %all-gather.13.cloned.1.call-start = ((), (), s32[]{:S(2)}) async-start(), calls=%async_computation.3 | async-start | bytes 1114112 | tf_op jit(solution)/shard_map/all_gather | solution.py:49
  62.3 171.7 %all-gather.15.cloned.1.call-start = ((), (), s32[]{:S(2)}) async-start(), calls=%async_computation.4 | async-start | bytes 4456448 | tf_op jit(solution)/shard_map/all_gather | solution.py:50
  62.9 213.1 %all-gather.17.cloned.1.call-start = ((), (), s32[]{:S(2)}) async-start(), calls=%async_computation.5 | async-start | bytes 2228224 | tf_op jit(solution)/shard_map/all_gather | solution.py:51
  147.3 35.2 %copy-start = (bf16[128,1024]{1,0:T(8,128)(2,1)S(1)}, bf16[128,1024]{1,0:T(8,128)(2,1)}, u32[]{:S(2)}) copy-start(bf16[128,1024]{1,0:T(8,128)(2,1)} %param.11) | copy-start | bytes 786436
  147.3 86.7 %copy-start.2 = (f32[1024]{0:T(1024)S(1)}, f32[1024]{0:T(1024)}, u32[]{:S(2)}) copy-start(f32[1024]{0:T(1024)} %param.16) | copy-start | bytes 12292
  184.1 56.5 %copy-start.1 = (f32[9,1024]{1,0:T(8,128)S(1)}, f32[9,1024]{1,0:T(8,128)}, u32[]{:S(2)}) copy-start(f32[9,1024]{1,0:T(8,128)} %param.18) | copy-start | bytes 110596
  184.1 91.8 %copy-start.3 = (f32[1024]{0:T(1024)S(1)}, f32[1024]{0:T(1024)}, u32[]{:S(2)}) copy-start(f32[1024]{0:T(1024)} %param.20) | copy-start | bytes 12292
  184.1 91.8 %copy-start.4 = (f32[1024]{0:T(1024)S(1)}, f32[1024]{0:T(1024)}, u32[]{:S(2)}) copy-start(f32[1024]{0:T(1024)} %param.19) | copy-start | bytes 12292
  237.1 3.5 %collective-permute-start = (bf16[4,1024]{1,0:T(4,128)(2,1)S(1)}, bf16[4,1024]{1,0:T(4,128)(2,1)S(1)}, u32[]{:S(2)}, u32[]{:S(2)}) collective-permute-start(bf16[4,1024]{1,0:T(4,128)(2,1)S(1)} %get-tuple-element.8), channel_id=1, source_target_pairs={{0,1},{1,2},{2,3},{3,4},{4,5},{5,6},{6,7},{7,8},{8,9},{9,10},{10,1... | collective-permute-start | bytes 24584 | tf_op jit(solution)/shard_map/ppermute | solution.py:23
  239.3 3.1 %collective-permute-start.1 = (bf16[4,1024]{1,0:T(4,128)(2,1)S(1)}, bf16[4,1024]{1,0:T(4,128)(2,1)S(1)}, u32[]{:S(2)}, u32[]{:S(2)}) collective-permute-start(bf16[4,1024]{1,0:T(4,128)(2,1)S(1)} %get-tuple-element.9), channel_id=1, source_target_pairs={{1,0},{2,1},{3,2},{4,3},{5,4},{6,5},{7,6},{8,7},{9,8},{10,9},{11,1... | collective-permute-start | bytes 24584 | tf_op jit(solution)/shard_map/ppermute | solution.py:25
Sparse Core Ops, SparseCore 0:
  9.6 47.8 all-gather.6
  61.1 40.1 all-gather.10
  103.5 40.1 all-gather.8
  145.7 36.7 all-gather.12
  184.5 49.4 all-gather.14
  236.0 39.8 all-gather.16
where the time goes:
time: 287 us; the launch traced here: 286 us
  waiting for transfers between devices  246 us (86%)
  matrix products  14.4 us (5%)
  between operations  14.3 us (5%)
  other arithmetic  3.81 us (1%)
  local copies, waits for them, and re-layouts  3.71 us (1%)
  starting transfers between devices  3.65 us (1%)
    all_gather x1, waiting for transfers between devices, per_device(): lax.all_gather(w_pw1, 'frames', axis=0, tiled=True)  49.6 us
    all_gather x1, waiting for transfers between devices, per_device(): lax.all_gather(w_qkv, 'frames', axis=0, tiled=True)  48 us
    all_gather x1, waiting for transfers between devices, per_device(): key_rows = lax.all_gather(keys, 'frames', axis=0, tiled=True)  39.4 us
    all_gather x1, waiting for transfers between devices, per_device(): value_rows = lax.all_gather(values, 'frames', axis=0, tiled=True)  37.2 us
    all_gather x1, waiting for transfers between devices, per_device(): lax.all_gather(w_out, 'frames', axis=0, tiled=True)  33.8 us
    all_gather x1, waiting for transfers between devices, per_device(): lax.all_gather(w_pw2, 'frames', axis=0, tiled=True)  33.5 us
  transfers between devices with their start and end apart: 8, of which 7 were waited for; matrix products, arithmetic and copies ran while one was open for 5% of the time, Pallas kernels for 0%

commit v1 on v0

--- a/solution.py
+++ b/solution.py
@@ -1,8 +1,11 @@
+import functools
 import math
 
 import jax
 import jax.numpy as jnp
 from jax import lax
+from jax.experimental import pallas as pl
+from jax.experimental.pallas import tpu as pltpu
 from jax.sharding import PartitionSpec as P
 
 HEADS = 4
@@ -37,7 +40,7 @@
     return (centred * lax.rsqrt(variance + EPSILON) * gain).astype(jnp.bfloat16)
 
 
-def per_device(
+def per_device_xla(
     features, valid_length, ln1_gain, w_qkv, w_out, ln2_gain, w_pw1, w_dw, bn_scale, bn_shift, w_pw2
 ):
     limit = valid_length[0]
@@ -111,6 +114,335 @@
     return result.astype(jnp.bfloat16)
 
 
+ZS = 4
+CHUNK = 256
+PAD = 16
+QKV, FEAT, OUT, PW1, PW2 = range(5)
+WHOLE, CROSS, SPLIT = range(3)
+KIND = (CROSS, WHOLE, CROSS, SPLIT, CROSS)
+
+
+def norm_rows(values, gain):
+    values = values.astype(jnp.float32)
+    mean = jnp.mean(values, axis=-1, keepdims=True)
+    centred = values - mean
+    variance = jnp.mean(centred * centred, axis=-1, keepdims=True)
+    return (centred * lax.rsqrt(variance + EPSILON) * gain).astype(jnp.bfloat16)
+
+
+def block_kernel(
+    limit_ref, feat_ref, ln1_ref, qkv_ref, out_w_ref, ln2_ref, pw1_ref, dw_ref, bns_ref, bnb_ref, pw2_ref,
+    result_ref,
+    g_qkv, g_feat, g_out, g_pw1, g_pw2, kv, rows_n, ext, ext_n, query, context, attended, gate, act,
+    local_sem, zp_send, zm_send, z_recv, y_send, y_recv, x_send, x_recv, c_send, c_recv,
+):
+    twin = lax.axis_index("groups")
+    me = lax.axis_index("frames")
+    z, y, c = me // 4, (me // 2) % 2, me % 2
+    gathered = (g_qkv, g_feat, g_out, g_pw1, g_pw2)
+    shards = (qkv_ref, feat_ref, out_w_ref, pw1_ref, pw2_ref)
+    above, below = {"frames": me + 4}, {"frames": me - 4}
+    across = {"frames": me + 2 - 4 * y}
+    core = {"frames": me + 1 - 2 * c}
+    other = {"groups": 1 - twin}
+    att = query.shape[1]
+    width = ext.shape[1]
+    local_rows = feat_ref.shape[0]
+
+    own = []
+    for q in range(5):
+        if KIND[q] == SPLIT:
+            own.append(
+                pltpu.make_async_copy(shards[q].at[twin], gathered[q].at[z, y, c, twin], local_sem.at[q])
+            )
+        else:
+            own.append(pltpu.make_async_copy(shards[q], gathered[q].at[z, y, c], local_sem.at[q]))
+        own[-1].start()
+
+    barrier = pltpu.get_barrier_semaphore()
+
+    def greet(device):
+        pl.semaphore_signal(barrier, inc=1, device_id=device, device_id_type=pl.DeviceIdType.MESH)
+
+    greet(across)
+    greet(core)
+    greet(other)
+    pl.when(z > 0)(lambda: greet(below))
+    pl.when(z < ZS - 1)(lambda: greet(above))
+    pl.semaphore_wait(
+        barrier, 3 + jnp.where(z > 0, 1, 0) + jnp.where(z < ZS - 1, 1, 0)
+    )
+
+    def remote(src, dst, send, recv, device):
+        return pltpu.make_async_remote_copy(
+            src_ref=src, dst_ref=dst, send_sem=send, recv_sem=recv,
+            device_id=device, device_id_type=pl.DeviceIdType.MESH,
+        )
+
+    def along_z(q, source, up):
+        part = gathered[q].at[source, y, c]
+        if KIND[q] == SPLIT:
+            part = part.at[twin]
+        send = zp_send if up else zm_send
+        return remote(part, part, send.at[q, source], z_recv.at[q, source], above if up else below)
+
+    def along_y(q, source, column):
+        part = gathered[q].at[source, column, c]
+        if KIND[q] != WHOLE:
+            part = part.at[twin]
+        return remote(part, part, y_send.at[q, source], y_recv.at[q, source], across)
+
+    def along_x(q, half):
+        if KIND[q] == SPLIT:
+            part = gathered[q].at[:, :, c, half]
+        else:
+            part = gathered[q].at[:, 1 - y, c, half]
+        return remote(part, part, x_send.at[q], x_recv.at[q], other)
+
+    def to_core(q, which):
+        part = gathered[q].at[:, :, which]
+        return remote(part, part, c_send.at[q], c_recv.at[q], core)
+
+    def begin(q):
+        own[q].wait()
+        pl.when(z < ZS - 1)(lambda: along_z(q, z, True).start())
+        pl.when(z > 0)(lambda: along_z(q, z, False).start())
+        along_y(q, z, y).start()
+
+    def pass_on(q, s):
+        @pl.when(z >= s)
+        def _():
+            source = z - s
+            along_z(q, source, True).wait_recv()
+            pl.when(z < ZS - 1)(lambda: along_z(q, source, True).start())
+            along_y(q, source, y).start()
+
+        @pl.when(z + s <= ZS - 1)
+        def _():
+            source = z + s
+            along_z(q, source, False).wait_recv()
+            pl.when(z > 0)(lambda: along_z(q, source, False).start())
+            along_y(q, source, y).start()
+
+    def cross(q):
+        for source in range(ZS):
+            along_y(q, source, 1 - y).wait_recv()
+        if KIND[q] == WHOLE:
+            to_core(q, c).start()
+        else:
+            along_x(q, twin).start()
+
+    def swap(q):
+        along_x(q, 1 - twin).wait_recv()
+        to_core(q, c).start()
+
+    def arrive(q):
+        to_core(q, 1 - c).wait_recv()
+
+    def finish(q):
+        pl.when(z < ZS - 1)(lambda: along_z(q, z, True).wait_send())
+        pl.when(z > 0)(lambda: along_z(q, z, False).wait_send())
+        for s in range(1, ZS):
+            pl.when((z >= s) & (z < ZS - 1))(lambda: along_z(q, z - s, True).wait_send())
+            pl.when((z + s <= ZS - 1) & (z > 0))(lambda: along_z(q, z + s, False).wait_send())
+        for source in range(ZS):
+            along_y(q, source, y).wait_send()
+        if KIND[q] != WHOLE:
+            along_x(q, twin).wait_send()
+        to_core(q, c).wait_send()
+
+    def columns(ref, start):
+        block = ref[:, :, :, :, :, pl.ds(start, CHUNK)]
+        return block.reshape(-1, CHUNK)
+
+    def at(j):
+        return pl.multiple_of(j * CHUNK, CHUNK)
+
+    def key_values(r):
+        rows_n[...] = norm_rows(g_feat[r].reshape(rows_n.shape), ln1_ref[...])
+
+        def some(j, carry):
+            product = jnp.dot(
+                rows_n[...], columns(g_qkv, at(j) + att), preferred_element_type=jnp.float32
+            )
+            kv[r, :, pl.ds(at(j), CHUNK)] = product.astype(jnp.bfloat16)
+            return carry
+
+        lax.fori_loop(0, 2 * att // CHUNK, some, 0)
+
+    def queries():
+        before = jnp.maximum(me - 1, 0)
+        after = jnp.minimum(me + 1, 4 * ZS - 1)
+        ext[pl.ds(0, PAD), :] = g_feat[before // 4, (before // 2) % 2, before % 2, pl.ds(local_rows - PAD, PAD), :]
+        ext[pl.ds(PAD, local_rows), :] = g_feat[z, y, c]
+        ext[pl.ds(PAD + local_rows, PAD), :] = g_feat[after // 4, (after // 2) % 2, after % 2, pl.ds(0, PAD), :]
+        ext_n[...] = norm_rows(ext[...], ln1_ref[...])
+
+        def some(j, carry):
+            product = jnp.dot(ext_n[...], columns(g_qkv, at(j)), preferred_element_type=jnp.float32)
+            query[:, pl.ds(at(j), CHUNK)] = product.astype(jnp.bfloat16)
+            return carry
+
+        lax.fori_loop(0, att // CHUNK, some, 0)
+
+    def attend(h):
+        keys = kv[:, :, pl.ds(h * HD, HD)].reshape(-1, HD)
+        scores = lax.dot_general(
+            query[:, pl.ds(h * HD, HD)], keys, (((1,), (1,)), ((), ())), preferred_element_type=jnp.float32
+        ) * (1.0 / math.sqrt(HD))
+        valid = lax.broadcasted_iota(jnp.int32, scores.shape, 1) < limit_ref[0]
+        scores = jnp.where(valid, scores, -1e30)
+        peak = jnp.max(scores, axis=-1, keepdims=True)
+        weights = jnp.where(valid, jnp.exp(scores - peak), 0.0)
+        totals = jnp.sum(weights, axis=-1, keepdims=True)
+        values = kv[:, :, pl.ds(att + h * HD, HD)].reshape(-1, HD)
+        summed = jnp.dot(weights.astype(jnp.bfloat16), values, preferred_element_type=jnp.float32)
+        context[:, pl.ds(h * HD, HD)] = (summed / totals).astype(jnp.bfloat16)
+
+    def project():
+        def some(j, carry):
+            product = jnp.dot(context[...], columns(g_out, at(j)), preferred_element_type=jnp.float32)
+            attended[:, pl.ds(at(j), CHUNK)] = ext[:, pl.ds(at(j), CHUNK)].astype(jnp.float32) + product
+            return carry
+
+        lax.fori_loop(0, width // CHUNK, some, 0)
+        ext_n[...] = norm_rows(attended[...], ln2_ref[...])
+
+    def convolve():
+        def some(j, carry):
+            value = jnp.dot(ext_n[...], columns(g_pw1, at(j)), preferred_element_type=jnp.float32)
+            gates = jnp.dot(ext_n[...], columns(g_pw1, at(j) + width), preferred_element_type=jnp.float32)
+            frame = me * local_rows - PAD + lax.broadcasted_iota(jnp.int32, value.shape, 0)
+            valid = (frame >= 0) & (frame < limit_ref[0])
+            gated = jnp.where(valid, value * jax.nn.sigmoid(gates), 0.0)
+            gate[...] = gated.astype(jnp.bfloat16).astype(jnp.float32)
+            taps = dw_ref.shape[0]
+            cols = pl.ds(at(j), CHUNK)
+            conv = jnp.zeros((local_rows, CHUNK), jnp.float32)
+            for tap in range(taps):
+                conv = conv + dw_ref[pl.ds(tap, 1), cols] * gate[pl.ds(PAD - taps // 2 + tap, local_rows), :]
+            shifted = bns_ref[:, cols] * conv + bnb_ref[:, cols]
+            act[:, cols] = (shifted / (1.0 + jnp.exp(-shifted))).astype(jnp.bfloat16)
+            return carry
+
+        lax.fori_loop(0, width // CHUNK, some, 0)
+
+    def close():
+        def some(j, carry):
+            cols = pl.ds(at(j), CHUNK)
+            product = jnp.dot(act[...], columns(g_pw2, at(j)), preferred_element_type=jnp.float32)
+            result_ref[:, cols] = (attended[pl.ds(PAD, local_rows), cols] + product).astype(jnp.bfloat16)
+            return carry
+
+        lax.fori_loop(0, width // CHUNK, some, 0)
+
+    begin(QKV)
+    begin(FEAT)
+    pass_on(QKV, 1)
+    pass_on(FEAT, 1)
+    pass_on(QKV, 2)
+    pass_on(FEAT, 2)
+    pass_on(QKV, 3)
+    begin(OUT)
+    pass_on(FEAT, 3)
+    begin(PW1)
+    cross(QKV)
+    cross(FEAT)
+    swap(QKV)
+    pass_on(OUT, 1)
+    arrive(QKV)
+    arrive(FEAT)
+    key_values(0)
+    pass_on(PW1, 1)
+    pass_on(OUT, 2)
+    begin(PW2)
+    key_values(1)
+    pass_on(PW1, 2)
+    pass_on(OUT, 3)
+    pass_on(PW2, 1)
+    key_values(2)
+    pass_on(PW1, 3)
+    pass_on(PW2, 2)
+    key_values(3)
+    cross(OUT)
+    pass_on(PW2, 3)
+    queries()
+    attend(0)
+    cross(PW1)
+    swap(OUT)
+    attend(1)
+    cross(PW2)
+    swap(PW1)
+    attend(2)
+    swap(PW2)
+    attend(3)
+    arrive(OUT)
+    project()
+    arrive(PW1)
+    convolve()
+    arrive(PW2)
+    close()
+    for q in range(5):
+        finish(q)
+
+
+def per_device_kernel(
+    features, valid_length, ln1_gain, w_qkv, w_out, ln2_gain, w_pw1, w_dw, bn_scale, bn_shift, w_pw2
+):
+    local_rows, width = features.shape
+    att = w_qkv.shape[1] // 3
+    wide = local_rows + 2 * PAD
+
+    def halves(weight):
+        return weight.reshape(2, weight.shape[0] // 2, weight.shape[1])
+
+    shards = [halves(w) for w in (w_qkv, w_out, w_pw1, w_pw2)]
+    grid = (ZS, 2, 2)
+    bf16, f32 = jnp.bfloat16, jnp.float32
+    dma = pltpu.SemaphoreType.DMA
+    hbm = pl.BlockSpec(memory_space=pl.ANY)
+    vmem = pl.BlockSpec(memory_space=pltpu.VMEM)
+    return pl.pallas_call(
+        block_kernel,
+        out_shape=jax.ShapeDtypeStruct((local_rows, width), bf16),
+        in_specs=[
+            pl.BlockSpec(memory_space=pltpu.SMEM), hbm, vmem, hbm, hbm, vmem, hbm, vmem, vmem, vmem, hbm,
+        ],
+        out_specs=vmem,
+        scratch_shapes=[
+            pltpu.VMEM(grid + shards[0].shape, bf16),
+            pltpu.VMEM(grid + features.shape, bf16),
+            pltpu.VMEM(grid + shards[1].shape, bf16),
+            pltpu.VMEM(grid + shards[2].shape, bf16),
+            pltpu.VMEM(grid + shards[3].shape, bf16),
+            pltpu.VMEM((ZS, 4 * local_rows, 2 * att), bf16),
+            pltpu.VMEM((4 * local_rows, width), bf16),
+            pltpu.VMEM((wide, width), bf16),
+            pltpu.VMEM((wide, width), bf16),
+            pltpu.VMEM((wide, att), bf16),
+            pltpu.VMEM((wide, att), bf16),
+            pltpu.VMEM((wide, width), f32),
+            pltpu.VMEM((wide, CHUNK), f32),
+            pltpu.VMEM((local_rows, width), bf16),
+            dma((5,)),
+        ]
+        + [dma((5, ZS))] * 5
+        + [dma((5,))] * 4,
+        compiler_params=pltpu.CompilerParams(
+            collective_id=0, has_side_effects=True, vmem_limit_bytes=56 * 1024 * 1024
+        ),
+    )(
+        valid_length, features, ln1_gain[None], shards[0], shards[1], ln2_gain[None], shards[2], w_dw,
+        bn_scale[None], bn_shift[None], shards[3],
+    )
+
+
+def per_device(*arguments):
+    if lax.axis_size("frames") == 4 * ZS and lax.axis_size("groups") == 2:
+        return per_device_kernel(*arguments)
+    return per_device_xla(*arguments)
+
+
 def solution(mesh):
     placed = (
         P(("groups", "frames"), None),

time: 287 us -> 104 us (0.36)
  waiting for transfers between devices: 246 us -> 0 us
  Pallas kernels: 0 us -> 101 us
  matrix products: 14.4 us -> 0 us
  between operations: 14.3 us -> 0.66 us
  other arithmetic: 3.81 us -> 0 us
  starting transfers between devices: 3.65 us -> 0 us
    all_gather x6 -> x0, waiting for transfers between devices: 242 us -> none  [the longest x1 49.6 us: per_device(): lax.all_gather(w_pw1, 'frames', axis=0, tiled=True)]
    pallas_call x0 -> x1, Pallas kernels: none -> 101 us  [per_device_kernel(): pl.pallas_call(block_kernel, out_shape=jax.ShapeDtypeStruct((local_rows,...]
    dot_general x6 -> x0, matrix products: 14.4 us -> none  [the longest x1 3.33 us: per_device(): jnp.dot(activated, full_pw2, preferred_element_type=jnp.float32)]
    reduce_sum x4 -> x0, other arithmetic: 3.53 us -> none  [the longest x2 1.37 us: layer_norm(): variance = jnp.mean(centred * centred, axis=-1, keepdims=True)]
    ppermute x2 -> x0, starting transfers between devices: 3.45 us -> none  [the longest x1 2.16 us: extended(): lax.ppermute(tail, axis, [(i, (i + 1) % count) for i in range(ends)])]
    unnamed x6 -> x0, waiting for transfers between devices: 2.99 us -> none
    reshape x1 -> x0, local copies, waits for them, and re-layouts: 2.93 us -> none  [per_device(): value_heads = value_rows.reshape(count, HEADS, HD)]
  transfers between devices with their start and end apart: 8 -> 0, of which waited for: 7 -> 0; matrix products, arithmetic and copies ran while one was open for 5% -> 0% of each run, Pallas kernels for 0% -> 0%
where the time goes in v1:
time: 104 us
  Pallas kernels  101 us (97%)
  local copies, waits for them, and re-layouts  1.67 us (2%)
    pallas_call x1, Pallas kernels, per_device_kernel(): pl.pallas_call(block_kernel, out_shape=jax.ShapeDtypeStruct((local_rows,...  101 us

profile of v1, /device:TPU:0, one launch (start us, length us, event | category | flops | bytes accessed | tf_op | source)
XLA Modules:
  0.0 103.6 jit_solution(5137173288249017132)
XLA Ops:
  0.7 101.3 %shard_map.109 = bf16[128,1024]{1,0:T(8,128)(2,1)} custom-call(s32[1]{0:T(128)S(6)} %copy.13.limit_ref, bf16[128,1024]{1,0:T(8,128)(2,1)} %feat_ref.1, f32[1,1024]{1,0:T(1,128)} %bitcast.12, bf16[2,32,1536]{2,1,0:T(8,128)(2,1)} %bitcast.9, bf16[2,16,1024]{2,1,0:T(8,128)(2,1)} %bitcast.11, f32[1,1024]{1,0:T(1,128)} %bitcast.13, bf16[2,32,2048]{2,1,0:T(8,128)(2,1)} %bitcast.8, ...), custom_call_target="tpu_custom_call" | custom-call | tf_op jit(solution)/shard_map/pallas_call | solution.py:405
  101.9 1.7 %copy.14 = bf16[128,1024]{1,0:T(8,128)(2,1)} copy(bf16[128,1024]{1,0:T(8,128)(2,1)} %shard_map.109) | data formatting | bytes 524288

commit v2 on v1

--- a/solution.py
+++ b/solution.py
@@ -117,9 +117,11 @@
 ZS = 4
 CHUNK = 256
 PAD = 16
-QKV, FEAT, OUT, PW1, PW2 = range(5)
-WHOLE, CROSS, SPLIT = range(3)
-KIND = (CROSS, WHOLE, CROSS, SPLIT, CROSS)
+HALO = 8
+KVW, FEAT, QW, OUT, PW1, PW2 = range(6)
+COLUMN, CROSS, SPLIT = range(3)
+KIND = (CROSS, COLUMN, CROSS, CROSS, SPLIT, CROSS)
+COUNT = len(KIND)
 
 
 def norm_rows(values, gain):
@@ -133,32 +135,38 @@
 def block_kernel(
     limit_ref, feat_ref, ln1_ref, qkv_ref, out_w_ref, ln2_ref, pw1_ref, dw_ref, bns_ref, bnb_ref, pw2_ref,
     result_ref,
-    g_qkv, g_feat, g_out, g_pw1, g_pw2, kv, rows_n, ext, ext_n, query, context, attended, gate, act,
-    local_sem, zp_send, zm_send, z_recv, y_send, y_recv, x_send, x_recv, c_send, c_recv,
+    g_kvw, g_feat, g_qw, g_out, g_pw1, g_pw2, kv, halo, rows_n, ext, ext_n, query, context, attended, gate, act,
+    local_sem, zp_send, zm_send, z_recv, y_send, y_recv, x_send, x_recv, c_send, c_recv, kvc_send, kvc_recv,
+    halo_send, halo_recv,
 ):
     twin = lax.axis_index("groups")
     me = lax.axis_index("frames")
     z, y, c = me // 4, (me // 2) % 2, me % 2
-    gathered = (g_qkv, g_feat, g_out, g_pw1, g_pw2)
-    shards = (qkv_ref, feat_ref, out_w_ref, pw1_ref, pw2_ref)
+    att = query.shape[1]
+    width = ext.shape[1]
+    local_rows = feat_ref.shape[0]
+    last = 4 * ZS - 1
+    gathered = (g_kvw, g_feat, g_qw, g_out, g_pw1, g_pw2)
+    shards = (
+        qkv_ref.at[:, :, pl.ds(att, 2 * att)], feat_ref, qkv_ref.at[:, :, pl.ds(0, att)], out_w_ref, pw1_ref, pw2_ref,
+    )
     above, below = {"frames": me + 4}, {"frames": me - 4}
     across = {"frames": me + 2 - 4 * y}
     core = {"frames": me + 1 - 2 * c}
     other = {"groups": 1 - twin}
-    att = query.shape[1]
-    width = ext.shape[1]
-    local_rows = feat_ref.shape[0]
 
     own = []
-    for q in range(5):
+    for q in range(COUNT):
         if KIND[q] == SPLIT:
             own.append(
                 pltpu.make_async_copy(shards[q].at[twin], gathered[q].at[z, y, c, twin], local_sem.at[q])
             )
         else:
-            own.append(pltpu.make_async_copy(shards[q], gathered[q].at[z, y, c], local_sem.at[q]))
+            part = gathered[q].at[z] if KIND[q] == COLUMN else gathered[q].at[z, y, c]
+            own.append(pltpu.make_async_copy(shards[q], part, local_sem.at[q]))
         own[-1].start()
 
+    halo[...] = jnp.zeros_like(halo)
     barrier = pltpu.get_barrier_semaphore()
 
     def greet(device):
@@ -169,9 +177,12 @@
     greet(other)
     pl.when(z > 0)(lambda: greet(below))
     pl.when(z < ZS - 1)(lambda: greet(above))
-    pl.semaphore_wait(
-        barrier, 3 + jnp.where(z > 0, 1, 0) + jnp.where(z < ZS - 1, 1, 0)
-    )
+    pl.when(me > 0)(lambda: greet({"frames": me - 1}))
+    pl.when(me < last)(lambda: greet({"frames": me + 1}))
+    greeted = 3
+    for there in (z > 0, z < ZS - 1, me > 0, me < last):
+        greeted = greeted + jnp.where(there, 1, 0)
+    pl.semaphore_wait(barrier, greeted)
 
     def remote(src, dst, send, recv, device):
         return pltpu.make_async_remote_copy(
@@ -180,16 +191,17 @@
         )
 
     def along_z(q, source, up):
-        part = gathered[q].at[source, y, c]
+        part = gathered[q].at[source] if KIND[q] == COLUMN else gathered[q].at[source, y, c]
         if KIND[q] == SPLIT:
             part = part.at[twin]
         send = zp_send if up else zm_send
         return remote(part, part, send.at[q, source], z_recv.at[q, source], above if up else below)
 
     def along_y(q, source, column):
-        part = gathered[q].at[source, column, c]
-        if KIND[q] != WHOLE:
-            part = part.at[twin]
+        if KIND[q] == COLUMN:
+            part = kv.at[source, column, c]
+        else:
+            part = gathered[q].at[source, column, c, twin]
         return remote(part, part, y_send.at[q, source], y_recv.at[q, source], across)
 
     def along_x(q, half):
@@ -207,7 +219,8 @@
         own[q].wait()
         pl.when(z < ZS - 1)(lambda: along_z(q, z, True).start())
         pl.when(z > 0)(lambda: along_z(q, z, False).start())
-        along_y(q, z, y).start()
+        if KIND[q] != COLUMN:
+            along_y(q, z, y).start()
 
     def pass_on(q, s):
         @pl.when(z >= s)
@@ -215,22 +228,21 @@
             source = z - s
             along_z(q, source, True).wait_recv()
             pl.when(z < ZS - 1)(lambda: along_z(q, source, True).start())
-            along_y(q, source, y).start()
+            if KIND[q] != COLUMN:
+                along_y(q, source, y).start()
 
         @pl.when(z + s <= ZS - 1)
         def _():
             source = z + s
             along_z(q, source, False).wait_recv()
             pl.when(z > 0)(lambda: along_z(q, source, False).start())
-            along_y(q, source, y).start()
+            if KIND[q] != COLUMN:
+                along_y(q, source, y).start()
 
     def cross(q):
         for source in range(ZS):
             along_y(q, source, 1 - y).wait_recv()
-        if KIND[q] == WHOLE:
-            to_core(q, c).start()
-        else:
-            along_x(q, twin).start()
+        along_x(q, twin).start()
 
     def swap(q):
         along_x(q, 1 - twin).wait_recv()
@@ -247,9 +259,27 @@
             pl.when((z + s <= ZS - 1) & (z > 0))(lambda: along_z(q, z + s, False).wait_send())
         for source in range(ZS):
             along_y(q, source, y).wait_send()
-        if KIND[q] != WHOLE:
+        if KIND[q] != COLUMN:
             along_x(q, twin).wait_send()
-        to_core(q, c).wait_send()
+            to_core(q, c).wait_send()
+
+    def kv_to_core(source, column, which):
+        part = kv.at[source, column, which]
+        slot = (source, column)
+        return remote(part, part, kvc_send.at[slot], kvc_recv.at[slot], core)
+
+    def in_round(s, do):
+        if s == 0:
+            do(z)
+        else:
+            pl.when(z >= s)(lambda: do(z - s))
+            pl.when(z + s <= ZS - 1)(lambda: do(z + s))
+
+    def edge(up):
+        rows = pl.ds(local_rows - PAD, PAD) if up else pl.ds(0, PAD)
+        slot = 0 if up else 1
+        device = {"frames": me + 1 if up else me - 1}
+        return remote(feat_ref.at[rows], halo.at[slot], halo_send.at[slot], halo_recv.at[slot], device)
 
     def columns(ref, start):
         block = ref[:, :, :, :, :, pl.ds(start, CHUNK)]
@@ -258,51 +288,55 @@
     def at(j):
         return pl.multiple_of(j * CHUNK, CHUNK)
 
-    def key_values(r):
-        rows_n[...] = norm_rows(g_feat[r].reshape(rows_n.shape), ln1_ref[...])
+    def key_values(source):
+        rows_n[...] = norm_rows(g_feat[source], ln1_ref[...])
 
         def some(j, carry):
-            product = jnp.dot(
-                rows_n[...], columns(g_qkv, at(j) + att), preferred_element_type=jnp.float32
-            )
-            kv[r, :, pl.ds(at(j), CHUNK)] = product.astype(jnp.bfloat16)
+            product = jnp.dot(rows_n[...], columns(g_kvw, at(j)), preferred_element_type=jnp.float32)
+            kv[source, y, c, :, pl.ds(at(j), CHUNK)] = product.astype(jnp.bfloat16)
             return carry
 
         lax.fori_loop(0, 2 * att // CHUNK, some, 0)
+        along_y(FEAT, source, y).start()
+        kv_to_core(source, y, c).start()
+
+    def kv_cross(source):
+        along_y(FEAT, source, 1 - y).wait_recv()
+        kv_to_core(source, 1 - y, c).start()
 
     def queries():
-        before = jnp.maximum(me - 1, 0)
-        after = jnp.minimum(me + 1, 4 * ZS - 1)
-        ext[pl.ds(0, PAD), :] = g_feat[before // 4, (before // 2) % 2, before % 2, pl.ds(local_rows - PAD, PAD), :]
-        ext[pl.ds(PAD, local_rows), :] = g_feat[z, y, c]
-        ext[pl.ds(PAD + local_rows, PAD), :] = g_feat[after // 4, (after // 2) % 2, after % 2, pl.ds(0, PAD), :]
+        pl.when(me > 0)(lambda: edge(True).wait_recv())
+        pl.when(me < last)(lambda: edge(False).wait_recv())
+        ext[pl.ds(0, HALO), :] = halo[0].astype(jnp.float32)[PAD - HALO :]
+        ext[pl.ds(HALO, local_rows), :] = g_feat[z].astype(jnp.float32)
+        ext[pl.ds(HALO + local_rows, HALO), :] = halo[1].astype(jnp.float32)[:HALO]
         ext_n[...] = norm_rows(ext[...], ln1_ref[...])
 
         def some(j, carry):
-            product = jnp.dot(ext_n[...], columns(g_qkv, at(j)), preferred_element_type=jnp.float32)
+            product = jnp.dot(ext_n[...], columns(g_qw, at(j)), preferred_element_type=jnp.float32)
             query[:, pl.ds(at(j), CHUNK)] = product.astype(jnp.bfloat16)
             return carry
 
         lax.fori_loop(0, att // CHUNK, some, 0)
 
     def attend(h):
-        keys = kv[:, :, pl.ds(h * HD, HD)].reshape(-1, HD)
+        keys = kv[:, :, :, :, pl.ds(h * HD, HD)].reshape(-1, HD)
         scores = lax.dot_general(
             query[:, pl.ds(h * HD, HD)], keys, (((1,), (1,)), ((), ())), preferred_element_type=jnp.float32
-        ) * (1.0 / math.sqrt(HD))
-        valid = lax.broadcasted_iota(jnp.int32, scores.shape, 1) < limit_ref[0]
-        scores = jnp.where(valid, scores, -1e30)
+        )
+        position = lax.broadcasted_iota(jnp.int32, (1, scores.shape[1]), 1)
+        scores = scores + jnp.where(position < limit_ref[0], 0.0, -1e30)
         peak = jnp.max(scores, axis=-1, keepdims=True)
-        weights = jnp.where(valid, jnp.exp(scores - peak), 0.0)
+        weights = jnp.exp2((scores - peak) * (math.log2(math.e) / math.sqrt(HD)))
         totals = jnp.sum(weights, axis=-1, keepdims=True)
-        values = kv[:, :, pl.ds(att + h * HD, HD)].reshape(-1, HD)
+        values = kv[:, :, :, :, pl.ds(att + h * HD, HD)].reshape(-1, HD)
         summed = jnp.dot(weights.astype(jnp.bfloat16), values, preferred_element_type=jnp.float32)
         context[:, pl.ds(h * HD, HD)] = (summed / totals).astype(jnp.bfloat16)
 
     def project():
         def some(j, carry):
             product = jnp.dot(context[...], columns(g_out, at(j)), preferred_element_type=jnp.float32)
-            attended[:, pl.ds(at(j), CHUNK)] = ext[:, pl.ds(at(j), CHUNK)].astype(jnp.float32) + product
+            attended[:, pl.ds(at(j), CHUNK)] = ext[:, pl.ds(at(j), CHUNK)] + product
             return carry
 
         lax.fori_loop(0, width // CHUNK, some, 0)
@@ -312,7 +346,7 @@
         def some(j, carry):
             value = jnp.dot(ext_n[...], columns(g_pw1, at(j)), preferred_element_type=jnp.float32)
             gates = jnp.dot(ext_n[...], columns(g_pw1, at(j) + width), preferred_element_type=jnp.float32)
-            frame = me * local_rows - PAD + lax.broadcasted_iota(jnp.int32, value.shape, 0)
+            frame = me * local_rows - HALO + lax.broadcasted_iota(jnp.int32, value.shape, 0)
             valid = (frame >= 0) & (frame < limit_ref[0])
             gated = jnp.where(valid, value * jax.nn.sigmoid(gates), 0.0)
             gate[...] = gated.astype(jnp.bfloat16).astype(jnp.float32)
@@ -320,7 +354,7 @@
             cols = pl.ds(at(j), CHUNK)
             conv = jnp.zeros((local_rows, CHUNK), jnp.float32)
             for tap in range(taps):
-                conv = conv + dw_ref[pl.ds(tap, 1), cols] * gate[pl.ds(PAD - taps // 2 + tap, local_rows), :]
+                conv = conv + dw_ref[pl.ds(tap, 1), cols] * gate[pl.ds(HALO - taps // 2 + tap, local_rows), :]
             shifted = bns_ref[:, cols] * conv + bnb_ref[:, cols]
             act[:, cols] = (shifted / (1.0 + jnp.exp(-shifted))).astype(jnp.bfloat16)
             return carry
@@ -331,47 +365,61 @@
         def some(j, carry):
             cols = pl.ds(at(j), CHUNK)
             product = jnp.dot(act[...], columns(g_pw2, at(j)), preferred_element_type=jnp.float32)
-            result_ref[:, cols] = (attended[pl.ds(PAD, local_rows), cols] + product).astype(jnp.bfloat16)
+            result_ref[:, cols] = (attended[pl.ds(HALO, local_rows), cols] + product).astype(jnp.bfloat16)
             return carry
 
         lax.fori_loop(0, width // CHUNK, some, 0)
 
-    begin(QKV)
+    begin(KVW)
     begin(FEAT)
-    pass_on(QKV, 1)
+    pl.when(me < last)(lambda: edge(True).start())
+    pl.when(me > 0)(lambda: edge(False).start())
+    pass_on(KVW, 1)
+    pass_on(KVW, 2)
     pass_on(FEAT, 1)
-    pass_on(QKV, 2)
+    pass_on(KVW, 3)
+    begin(QW)
+    begin(OUT)
+    cross(KVW)
+    swap(KVW)
     pass_on(FEAT, 2)
-    pass_on(QKV, 3)
-    begin(OUT)
+    begin(PW1)
+    arrive(KVW)
+    in_round(0, key_values)
+    in_round(1, key_values)
+    pass_on(QW, 1)
+    pass_on(OUT, 1)
+    in_round(2, key_values)
+    in_round(0, kv_cross)
     pass_on(FEAT, 3)
-    begin(PW1)
-    cross(QKV)
-    cross(FEAT)
-    swap(QKV)
-    pass_on(OUT, 1)
-    arrive(QKV)
-    arrive(FEAT)
-    key_values(0)
+    in_round(3, key_values)
+    begin(PW2)
+    pass_on(QW, 2)
+    pass_on(OUT, 2)
     pass_on(PW1, 1)
-    pass_on(OUT, 2)
-    begin(PW2)
-    key_values(1)
+    in_round(1, kv_cross)
+    pass_on(QW, 3)
+    pass_on(OUT, 3)
     pass_on(PW1, 2)
-    pass_on(OUT, 3)
     pass_on(PW2, 1)
-    key_values(2)
+    cross(QW)
+    in_round(2, kv_cross)
     pass_on(PW1, 3)
     pass_on(PW2, 2)
-    key_values(3)
+    swap(QW)
     cross(OUT)
+    in_round(3, kv_cross)
     pass_on(PW2, 3)
+    swap(OUT)
+    arrive(QW)
     queries()
+    for source in range(ZS):
+        for column in range(2):
+            kv_to_core(source, column, 1 - c).wait_recv()
+    cross(PW1)
     attend(0)
-    cross(PW1)
-    swap(OUT)
+    cross(PW2)
     attend(1)
-    cross(PW2)
     swap(PW1)
     attend(2)
     swap(PW2)
@@ -382,8 +430,14 @@
     convolve()
     arrive(PW2)
     close()
-    for q in range(5):
+
+    for q in range(COUNT):
         finish(q)
+    for source in range(ZS):
+        for column in range(2):
+            kv_to_core(source, column, c).wait_send()
+    pl.when(me < last)(lambda: edge(True).wait_send())
+    pl.when(me > 0)(lambda: edge(False).wait_send())
 
 
 def per_device_kernel(
@@ -391,7 +445,7 @@
 ):
     local_rows, width = features.shape
     att = w_qkv.shape[1] // 3
-    wide = local_rows + 2 * PAD
+    wide = local_rows + 2 * HALO
 
     def halves(weight):
         return weight.reshape(2, weight.shape[0] // 2, weight.shape[1])
@@ -410,24 +464,28 @@
         ],
         out_specs=vmem,
         scratch_shapes=[
-            pltpu.VMEM(grid + shards[0].shape, bf16),
-            pltpu.VMEM(grid + features.shape, bf16),
+            pltpu.VMEM(grid + shards[0].shape[:2] + (2 * att,), bf16),
+            pltpu.VMEM((ZS,) + features.shape, bf16),
+            pltpu.VMEM(grid + shards[0].shape[:2] + (att,), bf16),
             pltpu.VMEM(grid + shards[1].shape, bf16),
             pltpu.VMEM(grid + shards[2].shape, bf16),
             pltpu.VMEM(grid + shards[3].shape, bf16),
-            pltpu.VMEM((ZS, 4 * local_rows, 2 * att), bf16),
-            pltpu.VMEM((4 * local_rows, width), bf16),
-            pltpu.VMEM((wide, width), bf16),
+            pltpu.VMEM(grid + (local_rows, 2 * att), bf16),
+            pltpu.VMEM((2, PAD, width), bf16),
+            pltpu.VMEM((local_rows, width), bf16),
+            pltpu.VMEM((wide, width), f32),
             pltpu.VMEM((wide, width), bf16),
             pltpu.VMEM((wide, att), bf16),
             pltpu.VMEM((wide, att), bf16),
             pltpu.VMEM((wide, width), f32),
             pltpu.VMEM((wide, CHUNK), f32),
             pltpu.VMEM((local_rows, width), bf16),
-            dma((5,)),
+            dma((COUNT,)),
         ]
-        + [dma((5, ZS))] * 5
-        + [dma((5,))] * 4,
+        + [dma((COUNT, ZS))] * 5
+        + [dma((COUNT,))] * 4
+        + [dma((ZS, 2))] * 2
+        + [dma((2,))] * 2,
         compiler_params=pltpu.CompilerParams(
             collective_id=0, has_side_effects=True, vmem_limit_bytes=56 * 1024 * 1024
         ),

time: 104 us -> 116 us (1.12)
  Pallas kernels: 101 us -> 114 us
    pallas_call x1, Pallas kernels: 101 us -> 114 us  [per_device_kernel(): pl.pallas_call(block_kernel, out_shape=jax.ShapeDtypeStruct((local_rows,...]
where the time goes in v2:
time: 116 us
  Pallas kernels  114 us (98%)
  local copies, waits for them, and re-layouts  1.67 us (1%)
    pallas_call x1, Pallas kernels, per_device_kernel(): pl.pallas_call(block_kernel, out_shape=jax.ShapeDtypeStruct((local_rows,...  114 us

profile of v2, /device:TPU:0, one launch (start us, length us, event | category | flops | bytes accessed | tf_op | source)
XLA Modules:
  0.0 116.2 jit_solution(8130770187948205572)
XLA Ops:
  0.7 113.8 %shard_map.109 = bf16[128,1024]{1,0:T(8,128)(2,1)} custom-call(s32[1]{0:T(128)S(6)} %copy.13.limit_ref, bf16[128,1024]{1,0:T(8,128)(2,1)} %feat_ref.1, f32[1,1024]{1,0:T(1,128)} %bitcast.12, bf16[2,32,1536]{2,1,0:T(8,128)(2,1)} %bitcast.9, bf16[2,16,1024]{2,1,0:T(8,128)(2,1)} %bitcast.11, f32[1,1024]{1,0:T(1,128)} %bitcast.13, bf16[2,32,2048]{2,1,0:T(8,128)(2,1)} %bitcast.8, ...), custom_call_target="tpu_custom_call" | custom-call | tf_op jit(solution)/shard_map/pallas_call | solution.py:459
  114.5 1.7 %copy.14 = bf16[128,1024]{1,0:T(8,128)(2,1)} copy(bf16[128,1024]{1,0:T(8,128)(2,1)} %shard_map.109) | data formatting | bytes 524288

commit v3 on v1

v3 whole, which is shorter than its diff:
```python
import functools
import math

import jax
import jax.numpy as jnp
from jax import lax
from jax.experimental import pallas as pl
from jax.experimental.pallas import tpu as pltpu
from jax.sharding import PartitionSpec as P

HEADS = 4
HD = 128


EPSILON = 1e-05


def extended(cells, sides, width):
    for axis, dim in sides:
        count = lax.axis_size(axis)
        ends = count - 1
        head = lax.slice_in_dim(cells, 0, width, axis=dim)
        tail = lax.slice_in_dim(cells, cells.shape[dim] - width, cells.shape[dim], axis=dim)
        cells = jnp.concatenate(
            [
                lax.ppermute(tail, axis, [(i, (i + 1) % count) for i in range(ends)]),
                cells,
                lax.ppermute(head, axis, [((i + 1) % count, i) for i in range(ends)]),
            ],
            axis=dim,
        )
    return cells


def layer_norm(values, gain):
    values = values.astype(jnp.float32)
    mean = jnp.mean(values, axis=-1, keepdims=True)
    centred = values - mean
    variance = jnp.mean(centred * centred, axis=-1, keepdims=True)
    return (centred * lax.rsqrt(variance + EPSILON) * gain).astype(jnp.bfloat16)


def per_device_xla(
    features, valid_length, ln1_gain, w_qkv, w_out, ln2_gain, w_pw1, w_dw, bn_scale, bn_shift, w_pw2
):
    limit = valid_length[0]
    local_rows = features.shape[0]
    width = features.shape[1]
    att_width = w_qkv.shape[1] // 3
    scale = 1.0 / math.sqrt(HD)
    tails = (
        lax.all_gather(w_out, "frames", axis=0, tiled=True),
        lax.all_gather(w_pw1, "frames", axis=0, tiled=True),
        lax.all_gather(w_pw2, "frames", axis=0, tiled=True),
    )
    full_out, full_pw1, full_pw2 = tails
    normed1 = layer_norm(features, ln1_gain)
    qkv = jnp.dot(
        normed1,
        lax.all_gather(w_qkv, "frames", axis=0, tiled=True),
        preferred_element_type=jnp.float32,
    ).astype(jnp.bfloat16)
    query_heads = qkv[:, :att_width].reshape(local_rows, HEADS, HD)
    keys = qkv[:, att_width : 2 * att_width]
    values = qkv[:, 2 * att_width :]
    maxima = jnp.full((HEADS, local_rows), -1e30, jnp.float32)
    key_rows = lax.all_gather(keys, "frames", axis=0, tiled=True)
    value_rows = lax.all_gather(values, "frames", axis=0, tiled=True)
    count = key_rows.shape[0]
    key_heads = key_rows.reshape(count, HEADS, HD)
    value_heads = value_rows.reshape(count, HEADS, HD)
    scores = (
        jnp.einsum("qhd,khd->hqk", query_heads, key_heads, preferred_element_type=jnp.float32)
        * scale
    )
    position = jnp.arange(count, dtype=jnp.int32)
    valid = (position < limit)[None, None, :]
    scores = jnp.where(valid, scores, -1e30)
    fresh = jnp.maximum(maxima, jnp.max(scores, axis=-1))
    weights = jnp.where(valid, jnp.exp(scores - fresh[..., None]), 0.0)
    totals = jnp.sum(weights, axis=-1)
    update = jnp.einsum(
        "hqk,khd->hqd",
        weights.astype(jnp.bfloat16),
        value_heads,
        preferred_element_type=jnp.float32,
    )
    summed = update
    maxima, totals, summed = (fresh, totals, summed)
    context = (
        (summed / totals[..., None])
        .transpose(1, 0, 2)
        .reshape(local_rows, att_width)
        .astype(jnp.bfloat16)
    )
    attended = features.astype(jnp.float32) + jnp.dot(
        context, full_out, preferred_element_type=jnp.float32
    )
    normed2 = layer_norm(attended, ln2_gain)
    both = jnp.dot(normed2, full_pw1, preferred_element_type=jnp.float32)
    frame_index = lax.axis_index("frames") * local_rows + jnp.arange(local_rows, dtype=jnp.int32)
    frame_valid = (frame_index < limit)[:, None]
    gated = jnp.where(frame_valid, both[:, :width] * jax.nn.sigmoid(both[:, width:]), 0.0).astype(
        jnp.bfloat16
    )
    half_window = (w_dw.shape[0] - 1) // 2
    widened = extended(gated, (("frames", 0),), half_window)
    widened = widened.astype(jnp.float32)
    conv = jnp.zeros((local_rows, width), jnp.float32)
    for tap in range(w_dw.shape[0]):
        conv = conv + w_dw[tap][None, :] * widened[tap : tap + local_rows]
    activated = jax.nn.silu(bn_scale * conv + bn_shift).astype(jnp.bfloat16)
    result = attended + jnp.dot(activated, full_pw2, preferred_element_type=jnp.float32)
    return result.astype(jnp.bfloat16)


ZS = 4
QUAD = 4
CHUNK = 256
PAD = 16
HALO = 8
BLOCK = 176
OUT, PW1, PW2 = range(3)
COUNT = 3


def norm_rows(values, gain):
    values = values.astype(jnp.float32)
    mean = jnp.mean(values, axis=-1, keepdims=True)
    centred = values - mean
    variance = jnp.mean(centred * centred, axis=-1, keepdims=True)
    return (centred * lax.rsqrt(variance + EPSILON) * gain).astype(jnp.bfloat16)


def block_kernel(
    limit_ref, feat_ref, ln1_ref, qkv_ref, out_w_ref, ln2_ref, pw1_ref, dw_ref, bns_ref, bnb_ref, pw2_ref,
    result_ref,
    stage, g_qkv, g_feat, kv, g_out, g_pw1, g_pw2, rows_n, query, ctx, ctx_out, g_ctx, context, ext, ext_n, attended,
    gate, act,
    local_sem, zp_send, zm_send, z_recv, y_send, y_recv, x_send, x_recv, c_send, c_recv,
    peer_send, peer_recv, feat_send, feat_recv, edge_send, edge_recv, chain_p, chain_m, chain_recv,
):
    twin = lax.axis_index("groups")
    me = lax.axis_index("frames")
    z, y, c = me // 4, (me // 2) % 2, me % 2
    p = me % QUAD
    width = ext.shape[1]
    local_rows = feat_ref.shape[0]
    quad_rows = QUAD * local_rows
    gathered = (g_out, g_pw1, g_pw2)
    shards = (out_w_ref, pw1_ref, pw2_ref)
    above, below = {"frames": me + 4}, {"frames": me - 4}
    partners = (QUAD // 2 * (1 - y) + c, 2 * y + 1 - c, QUAD // 2 * (1 - y) + 1 - c)
    quad = [{"frames": z * QUAD + partner} for partner in partners]
    across, core = quad[0], quad[1]
    other = {"groups": 1 - twin}

    own = [
        pltpu.make_async_copy(shards[q].at[twin], gathered[q].at[z, y, c, twin], local_sem.at[q])
        for q in range(COUNT)
    ]
    own_feat = pltpu.make_async_copy(feat_ref, g_feat.at[p + 1], local_sem.at[COUNT])
    for copy in own + [own_feat]:
        copy.start()
    for head in range(QUAD):
        for kind in range(3):
            stage[head, :, pl.ds(kind * HD, HD)] = qkv_ref[:, pl.ds((kind * QUAD + head) * HD, HD)]
    g_qkv[z, p] = stage[p]
    g_feat[0, pl.ds(local_rows - PAD, PAD), :] = jnp.zeros((PAD, width), jnp.bfloat16)
    g_feat[QUAD + 1, pl.ds(0, PAD), :] = jnp.zeros((PAD, width), jnp.bfloat16)

    barrier = pltpu.get_barrier_semaphore()

    def greet(device):
        pl.semaphore_signal(barrier, inc=1, device_id=device, device_id_type=pl.DeviceIdType.MESH)

    for device in quad:
        greet(device)
    greet(other)
    pl.when(z > 0)(lambda: greet(below))
    pl.when(z < ZS - 1)(lambda: greet(above))
    pl.semaphore_wait(barrier, 4 + jnp.where(z > 0, 1, 0) + jnp.where(z < ZS - 1, 1, 0))

    def remote(src, dst, send, recv, device):
        return pltpu.make_async_remote_copy(
            src_ref=src, dst_ref=dst, send_sem=send, recv_sem=recv,
            device_id=device, device_id_type=pl.DeviceIdType.MESH,
        )

    def along_z(q, source, up):
        part = gathered[q].at[source, y, c, twin]
        send = zp_send if up else zm_send
        return remote(part, part, send.at[q, source], z_recv.at[q, source], above if up else below)

    def along_y(q, source, column):
        part = gathered[q].at[source, column, c, twin]
        return remote(part, part, y_send.at[q, source], y_recv.at[q, source], across)

    def along_x(q, half):
        part = gathered[q].at[:, :, c, half]
        return remote(part, part, x_send.at[q], x_recv.at[q], other)

    def to_core(q, which):
        part = gathered[q].at[:, :, which]
        return remote(part, part, c_send.at[q], c_recv.at[q], core)

    def chain(i, source, up):
        part = (g_qkv, kv)[i].at[source]
        send = chain_p if up else chain_m
        return remote(part, part, send.at[i, source], chain_recv.at[i, source], above if up else below)

    def columns_to(i, sender, receiver):
        return remote(stage.at[receiver], g_qkv.at[z, sender], peer_send.at[0, i], peer_recv.at[0, i], quad[i])

    def features_to(i, block):
        part = g_feat.at[block + 1]
        return remote(part, part, feat_send.at[i], feat_recv.at[i], across if i == 0 else core)

    def context_to(i, sender, receiver):
        rows = pl.ds(pl.multiple_of(receiver * local_rows, local_rows), local_rows + 2 * HALO)
        return remote(ctx_out.at[rows], g_ctx.at[sender], peer_send.at[1, i], peer_recv.at[1, i], quad[i])

    def edge(up):
        rows = pl.ds(local_rows - PAD, PAD) if up else pl.ds(0, PAD)
        src, dst = (QUAD, 0) if up else (1, QUAD + 1)
        slot = 0 if up else 1
        return remote(
            g_feat.at[src, rows], g_feat.at[dst, rows], edge_send.at[slot], edge_recv.at[slot],
            above if up else below,
        )

    def spread(piece, item):
        pl.when(z < ZS - 1)(lambda: piece(item, z, True).start())
        pl.when(z > 0)(lambda: piece(item, z, False).start())

    def onward(piece, item, s, after=None):
        @pl.when(z >= s)
        def _():
            piece(item, z - s, True).wait_recv()
            pl.when(z < ZS - 1)(lambda: piece(item, z - s, True).start())
            if after is not None:
                after(z - s)

        @pl.when(z + s <= ZS - 1)
        def _():
            piece(item, z + s, False).wait_recv()
            pl.when(z > 0)(lambda: piece(item, z + s, False).start())
            if after is not None:
                after(z + s)

    def sent(piece, item):
        for s in range(ZS):
            pl.when((z >= s) & (z < ZS - 1))(lambda: piece(item, z - s, True).wait_send())
            if s == 0:
                pl.when(z > 0)(lambda: piece(item, z, False).wait_send())
            else:
                pl.when((z + s <= ZS - 1) & (z > 0))(lambda: piece(item, z + s, False).wait_send())

    def begin(q):
        own[q].wait()
        spread(along_z, q)
        along_y(q, z, y).start()

    def pass_on(q, s):
        onward(along_z, q, s, lambda source: along_y(q, source, y).start())

    def cross(q):
        for source in range(ZS):
            along_y(q, source, 1 - y).wait_recv()
        along_x(q, twin).start()

    def swap(q):
        along_x(q, 1 - twin).wait_recv()
        to_core(q, c).start()

    def arrive(q):
        to_core(q, 1 - c).wait_recv()

    def finish(q):
        sent(along_z, q)
        for source in range(ZS):
            along_y(q, source, y).wait_send()
        along_x(q, twin).wait_send()
        to_core(q, c).wait_send()

    def columns(ref, start):
        block = ref[:, :, :, :, :, pl.ds(start, CHUNK)]
        return block.reshape(-1, CHUNK)

    def at(j):
        return pl.multiple_of(j * CHUNK, CHUNK)

    def normalise():
        def some(i, carry):
            rows_n[pl.ds(pl.multiple_of(i * local_rows, local_rows), local_rows), :] = norm_rows(
                g_feat[i + 1], ln1_ref[...]
            )
            return carry

        lax.fori_loop(0, QUAD, some, 0)

    def key_values():
        weight = g_qkv[:, :, :, pl.ds(HD, 2 * HD)].reshape(-1, 2 * HD)
        kv[z] = jnp.dot(rows_n[...], weight, preferred_element_type=jnp.float32).astype(jnp.bfloat16)

    def queries():
        weight = g_qkv[:, :, :, pl.ds(0, HD)].reshape(-1, HD)
        query[pl.ds(0, quad_rows), :] = jnp.dot(
            rows_n[...], weight, preferred_element_type=jnp.float32
        ).astype(jnp.bfloat16)
        pl.when(z > 0)(lambda: edge(True).wait_recv())
        pl.when(z < ZS - 1)(lambda: edge(False).wait_recv())
        before = g_feat[0, pl.ds(local_rows - PAD, PAD), :].astype(jnp.float32)[PAD - HALO :]
        after = g_feat[QUAD + 1, pl.ds(0, PAD), :].astype(jnp.float32)[:HALO]
        edges = norm_rows(jnp.concatenate([before, after], axis=0), ln1_ref[...])
        query[pl.ds(quad_rows, 2 * HALO), :] = jnp.dot(
            edges, weight, preferred_element_type=jnp.float32
        ).astype(jnp.bfloat16)
        before = g_feat[p, pl.ds(local_rows - PAD, PAD), :].astype(jnp.float32)[PAD - HALO :]
        after = g_feat[p + 2, pl.ds(0, PAD), :].astype(jnp.float32)[:HALO]
        ext[pl.ds(0, HALO), :] = before
        ext[pl.ds(HALO, local_rows), :] = g_feat[p + 1].astype(jnp.float32)
        ext[pl.ds(HALO + local_rows, HALO), :] = after

    def attend(i):
        rows = pl.ds(i * BLOCK, BLOCK)
        keys = kv[:, :, pl.ds(0, HD)].reshape(-1, HD)
        scores = lax.dot_general(
            query[rows, :], keys, (((1,), (1,)), ((), ())), preferred_element_type=jnp.float32
        )
        position = lax.broadcasted_iota(jnp.int32, (1, scores.shape[1]), 1)
        scores = scores + jnp.where(position < limit_ref[0], 0.0, -1e30)
        peak = jnp.max(scores, axis=-1, keepdims=True)
        weights = jnp.exp2((scores - peak) * (math.log2(math.e) / math.sqrt(HD)))
        totals = jnp.sum(weights, axis=-1, keepdims=True)
        values = kv[:, :, pl.ds(HD, HD)].reshape(-1, HD)
        summed = jnp.dot(weights.astype(jnp.bfloat16), values, preferred_element_type=jnp.float32)
        ctx[rows, :] = summed / totals

    def share_context():
        ctx_out[...] = jnp.concatenate(
            [ctx[pl.ds(quad_rows, HALO), :], ctx[pl.ds(0, quad_rows), :], ctx[pl.ds(quad_rows + HALO, HALO), :]], axis=0
        ).astype(jnp.bfloat16)
        for i, partner in enumerate(partners):
            context_to(i, p, partner).start()
        rows = pl.ds(pl.multiple_of(p * local_rows, local_rows), local_rows + 2 * HALO)
        g_ctx[p] = ctx_out[rows, :]

    def collect_context():
        for i, partner in enumerate(partners):
            context_to(i, partner, p).wait_recv()
        for head in range(QUAD):
            context[:, pl.ds(head * HD, HD)] = g_ctx[head]

    def project():
        def some(j, carry):
            product = jnp.dot(context[...], columns(g_out, at(j)), preferred_element_type=jnp.float32)
            attended[:, pl.ds(at(j), CHUNK)] = ext[:, pl.ds(at(j), CHUNK)] + product
            return carry

        lax.fori_loop(0, width // CHUNK, some, 0)
        ext_n[...] = norm_rows(attended[...], ln2_ref[...])

    def convolve():
        def some(j, carry):
            value = jnp.dot(ext_n[...], columns(g_pw1, at(j)), preferred_element_type=jnp.float32)
            gates = jnp.dot(ext_n[...], columns(g_pw1, at(j) + width), preferred_element_type=jnp.float32)
            frame = me * local_rows - HALO + lax.broadcasted_iota(jnp.int32, value.shape, 0)
            valid = (frame >= 0) & (frame < limit_ref[0])
            gated = jnp.where(valid, value * jax.nn.sigmoid(gates), 0.0)
            gate[...] = gated.astype(jnp.bfloat16).astype(jnp.float32)
            taps = dw_ref.shape[0]
            cols = pl.ds(at(j), CHUNK)
            conv = jnp.zeros((local_rows, CHUNK), jnp.float32)
            for tap in range(taps):
                conv = conv + dw_ref[pl.ds(tap, 1), cols] * gate[pl.ds(HALO - taps // 2 + tap, local_rows), :]
            shifted = bns_ref[:, cols] * conv + bnb_ref[:, cols]
            act[:, cols] = (shifted / (1.0 + jnp.exp(-shifted))).astype(jnp.bfloat16)
            return carry

        lax.fori_loop(0, width // CHUNK, some, 0)

    def close():
        def some(j, carry):
            cols = pl.ds(at(j), CHUNK)
            product = jnp.dot(act[...], columns(g_pw2, at(j)), preferred_element_type=jnp.float32)
            result_ref[:, cols] = (attended[pl.ds(HALO, local_rows), cols] + product).astype(jnp.bfloat16)
            return carry

        lax.fori_loop(0, width // CHUNK, some, 0)

    for i, partner in enumerate(partners):
        columns_to(i, p, partner).start()
    own_feat.wait()
    features_to(0, p).start()
    features_to(1, p).start()
    begin(OUT)
    for i, partner in enumerate(partners):
        columns_to(i, partner, p).wait_recv()
    spread(chain, 0)
    features_to(0, partners[0]).wait_recv()
    features_to(2, partners[0]).start()
    begin(PW1)
    features_to(1, partners[1]).wait_recv()
    features_to(2, partners[2]).wait_recv()
    pl.when(z < ZS - 1)(lambda: edge(True).start())
    pl.when(z > 0)(lambda: edge(False).start())
    onward(chain, 0, 1)
    pass_on(OUT, 1)
    normalise()
    onward(chain, 0, 2)
    pass_on(OUT, 2)
    pass_on(PW1, 1)
    onward(chain, 0, 3)
    key_values()
    spread(chain, 1)
    begin(PW2)
    queries()
    pass_on(OUT, 3)
    pass_on(PW1, 2)
    onward(chain, 1, 1)
    cross(OUT)
    pass_on(PW1, 3)
    pass_on(PW2, 1)
    onward(chain, 1, 2)
    swap(OUT)
    pass_on(PW2, 2)
    onward(chain, 1, 3)
    attend(0)
    cross(PW1)
    pass_on(PW2, 3)
    attend(1)
    cross(PW2)
    attend(2)
    share_context()
    swap(PW1)
    swap(PW2)
    arrive(OUT)
    collect_context()
    project()
    arrive(PW1)
    convolve()
    arrive(PW2)
    close()

    for q in range(COUNT):
        finish(q)
    for i in range(2):
        sent(chain, i)
    for i, partner in enumerate(partners):
        columns_to(i, p, partner).wait_send()
        context_to(i, p, partner).wait_send()
    for i, block in enumerate((p, p, partners[0])):
        features_to(i, block).wait_send()
    pl.when(z < ZS - 1)(lambda: edge(True).wait_send())
    pl.when(z > 0)(lambda: edge(False).wait_send())


def per_device_kernel(
    features, valid_length, ln1_gain, w_qkv, w_out, ln2_gain, w_pw1, w_dw, bn_scale, bn_shift, w_pw2
):
    local_rows, width = features.shape
    att = w_qkv.shape[1] // 3
    wide = local_rows + 2 * HALO

    def halves(weight):
        return weight.reshape(2, weight.shape[0] // 2, weight.shape[1])

    shards = [halves(w) for w in (w_out, w_pw1, w_pw2)]
    grid = (ZS, 2, 2)
    bf16, f32 = jnp.bfloat16, jnp.float32
    dma = pltpu.SemaphoreType.DMA
    hbm = pl.BlockSpec(memory_space=pl.ANY)
    vmem = pl.BlockSpec(memory_space=pltpu.VMEM)
    return pl.pallas_call(
        block_kernel,
        out_shape=jax.ShapeDtypeStruct((local_rows, width), bf16),
        in_specs=[
            pl.BlockSpec(memory_space=pltpu.SMEM), hbm, vmem, vmem, hbm, vmem, hbm, vmem, vmem, vmem, hbm,
        ],
        out_specs=vmem,
        scratch_shapes=[
            pltpu.VMEM((QUAD, w_qkv.shape[0], 3 * HD), bf16),
            pltpu.VMEM((ZS, QUAD, w_qkv.shape[0], 3 * HD), bf16),
            pltpu.VMEM((QUAD + 2, local_rows, width), bf16),
            pltpu.VMEM((ZS, QUAD * local_rows, 2 * HD), bf16),
            pltpu.VMEM(grid + shards[0].shape, bf16),
            pltpu.VMEM(grid + shards[1].shape, bf16),
            pltpu.VMEM(grid + shards[2].shape, bf16),
            pltpu.VMEM((QUAD * local_rows, width), bf16),
            pltpu.VMEM((QUAD * local_rows + 2 * HALO, HD), bf16),
            pltpu.VMEM((QUAD * local_rows + 2 * HALO, HD), f32),
            pltpu.VMEM((QUAD * local_rows + 2 * HALO, HD), bf16),
            pltpu.VMEM((QUAD, wide, HD), bf16),
            pltpu.VMEM((wide, att), bf16),
            pltpu.VMEM((wide, width), f32),
            pltpu.VMEM((wide, width), bf16),
            pltpu.VMEM((wide, width), f32),
            pltpu.VMEM((wide, CHUNK), f32),
            pltpu.VMEM((local_rows, width), bf16),
            dma((COUNT + 1,)),
        ]
        + [dma((COUNT, ZS))] * 5
        + [dma((COUNT,))] * 4
        + [dma((2, 3))] * 2
        + [dma((3,))] * 2
        + [dma((2,))] * 2
        + [dma((2, ZS))] * 3,
        compiler_params=pltpu.CompilerParams(
            collective_id=0, has_side_effects=True, vmem_limit_bytes=56 * 1024 * 1024
        ),
    )(
        valid_length, features, ln1_gain[None], w_qkv, shards[0], ln2_gain[None], shards[1], w_dw,
        bn_scale[None], bn_shift[None], shards[2],
    )


def per_device(*arguments):
    if lax.axis_size("frames") == 4 * ZS and lax.axis_size("groups") == 2:
        return per_device_kernel(*arguments)
    return per_device_xla(*arguments)


def solution(mesh):
    placed = (
        P(("groups", "frames"), None),
        P("groups"),
        P(),
        P("frames", None),
        P("frames", None),
        P(),
        P("frames", None),
        P(),
        P(),
        P(),
        P("frames", None),
    )
    return jax.shard_map(
        per_device,
        mesh=mesh,
        in_specs=placed,
        out_specs=P(("groups", "frames"), None),
        check_vma=False,
    )
```

time: 104 us -> 99.9 us (0.961)
  Pallas kernels: 101 us -> 97.4 us
    pallas_call x1, Pallas kernels: 101 us -> 97.4 us  [per_device_kernel(): pl.pallas_call(block_kernel, out_shape=jax.ShapeDtypeStruct((local_rows,...]
where the time goes in v3:
time: 99.9 us; the launch traced here: 99.7 us
  Pallas kernels  97.4 us (97%)
  local copies, waits for them, and re-layouts  1.67 us (2%)
    pallas_call x1, Pallas kernels, per_device_kernel(): pl.pallas_call(block_kernel, out_shape=jax.ShapeDtypeStruct((local_rows,...  97.4 us

profile of v3, /device:TPU:0, one launch (start us, length us, event | category | flops | bytes accessed | tf_op | source)
XLA Modules:
  0.0 99.7 jit_solution(45329436590930833)
XLA Ops:
  0.7 97.4 %shard_map.109 = bf16[128,1024]{1,0:T(8,128)(2,1)} custom-call(s32[1]{0:T(128)S(6)} %copy.13.limit_ref, bf16[128,1024]{1,0:T(8,128)(2,1)} %feat_ref.1, f32[1,1024]{1,0:T(1,128)} %bitcast.10, bf16[64,1536]{1,0:T(8,128)(2,1)} %qkv_ref.1, bf16[2,16,1024]{2,1,0:T(8,128)(2,1)} %bitcast.9, f32[1,1024]{1,0:T(1,128)} %bitcast.11, bf16[2,32,2048]{2,1,0:T(8,128)(2,1)} %bitcast.7, ...), custom_call_target="tpu_custom_call" | custom-call | tf_op jit(solution)/shard_map/pallas_call | solution.py:475
  98.1 1.7 %copy.14 = bf16[128,1024]{1,0:T(8,128)(2,1)} copy(bf16[128,1024]{1,0:T(8,128)(2,1)} %shard_map.109) | data formatting | bytes 524288

commit v4 on v3

--- a/solution.py
+++ b/solution.py
@@ -135,7 +135,7 @@
 def block_kernel(
     limit_ref, feat_ref, ln1_ref, qkv_ref, out_w_ref, ln2_ref, pw1_ref, dw_ref, bns_ref, bnb_ref, pw2_ref,
     result_ref,
-    stage, g_qkv, g_feat, kv, g_out, g_pw1, g_pw2, rows_n, query, ctx, ctx_out, g_ctx, context, ext, ext_n, attended,
+    stage, g_qkv, g_feat, kv, g_out, g_pw1, g_pw2, rows_n, query, ctx, peaks, totals, ctx_out, g_ctx, context, ext, ext_n, attended,
     gate, act,
     local_sem, zp_send, zm_send, z_recv, y_send, y_recv, x_send, x_recv, c_send, c_recv,
     peer_send, peer_recv, feat_send, feat_recv, edge_send, edge_recv, chain_p, chain_m, chain_recv,
@@ -156,7 +156,7 @@
     other = {"groups": 1 - twin}
 
     own = [
-        pltpu.make_async_copy(shards[q].at[twin], gathered[q].at[z, y, c, twin], local_sem.at[q])
+        pltpu.make_async_copy(shards[q], gathered[q].at[z, y, c], local_sem.at[q])
         for q in range(COUNT)
     ]
     own_feat = pltpu.make_async_copy(feat_ref, g_feat.at[p + 1], local_sem.at[COUNT])
@@ -196,13 +196,18 @@
         part = gathered[q].at[source, column, c, twin]
         return remote(part, part, y_send.at[q, source], y_recv.at[q, source], across)
 
-    def along_x(q, half):
-        part = gathered[q].at[:, :, c, half]
-        return remote(part, part, x_send.at[q], x_recv.at[q], other)
-
-    def to_core(q, which):
-        part = gathered[q].at[:, :, which]
-        return remote(part, part, c_send.at[q], c_recv.at[q], core)
+    def own_along_y(q, column):
+        part = gathered[q].at[z, column, c]
+        return remote(part, part, y_send.at[q, z], y_recv.at[q, z], across)
+
+    def along_x(q, source, column, half):
+        part = gathered[q].at[source, column, c, half]
+        slot = (q, source, column)
+        return remote(part, part, x_send.at[slot], x_recv.at[slot], other)
+
+    def to_core(q, which, half):
+        part = gathered[q].at[:, :, which, half]
+        return remote(part, part, c_send.at[q, half], c_recv.at[q, half], core)
 
     def chain(i, source, up):
         part = (g_qkv, kv)[i].at[source]
@@ -256,32 +261,57 @@
             else:
                 pl.when((z + s <= ZS - 1) & (z > 0))(lambda: piece(item, z + s, False).wait_send())
 
+    def in_round(s, do):
+        pl.when(z >= s)(lambda: do(z - s))
+        pl.when(z + s <= ZS - 1)(lambda: do(z + s))
+
     def begin(q):
         own[q].wait()
         spread(along_z, q)
-        along_y(q, z, y).start()
+        own_along_y(q, y).start()
 
     def pass_on(q, s):
-        onward(along_z, q, s, lambda source: along_y(q, source, y).start())
-
-    def cross(q):
-        for source in range(ZS):
+        def after(source):
+            along_y(q, source, y).start()
+            along_x(q, source, y, twin).start()
+
+        onward(along_z, q, s, after)
+
+    def cross(q, s):
+        def do(source):
             along_y(q, source, 1 - y).wait_recv()
-        along_x(q, twin).start()
+            along_x(q, source, 1 - y, twin).start()
+
+        in_round(s, do)
+        if s == ZS - 1:
+            own_along_y(q, 1 - y).wait_recv()
+            to_core(q, c, twin).start()
 
     def swap(q):
-        along_x(q, 1 - twin).wait_recv()
-        to_core(q, c).start()
+        def do(source):
+            for column in range(2):
+                along_x(q, source, column, 1 - twin).wait_recv()
+
+        for s in range(1, ZS):
+            in_round(s, do)
+        to_core(q, c, 1 - twin).start()
 
     def arrive(q):
-        to_core(q, 1 - c).wait_recv()
+        for half in range(2):
+            to_core(q, 1 - c, half).wait_recv()
 
     def finish(q):
+        def do(source):
+            along_y(q, source, y).wait_send()
+            for column in range(2):
+                along_x(q, source, column, twin).wait_send()
+
         sent(along_z, q)
-        for source in range(ZS):
-            along_y(q, source, y).wait_send()
-        along_x(q, twin).wait_send()
-        to_core(q, c).wait_send()
+        own_along_y(q, y).wait_send()
+        for s in range(1, ZS):
+            in_round(s, do)
+        for half in range(2):
+            to_core(q, c, half).wait_send()
 
     def columns(ref, start):
         block = ref[:, :, :, :, :, pl.ds(start, CHUNK)]
@@ -322,20 +352,39 @@
         ext[pl.ds(HALO, local_rows), :] = g_feat[p + 1].astype(jnp.float32)
         ext[pl.ds(HALO + local_rows, HALO), :] = after
 
-    def attend(i):
-        rows = pl.ds(i * BLOCK, BLOCK)
-        keys = kv[:, :, pl.ds(0, HD)].reshape(-1, HD)
-        scores = lax.dot_general(
-            query[rows, :], keys, (((1,), (1,)), ((), ())), preferred_element_type=jnp.float32
-        )
-        position = lax.broadcasted_iota(jnp.int32, (1, scores.shape[1]), 1)
-        scores = scores + jnp.where(position < limit_ref[0], 0.0, -1e30)
-        peak = jnp.max(scores, axis=-1, keepdims=True)
-        weights = jnp.exp2((scores - peak) * (math.log2(math.e) / math.sqrt(HD)))
-        totals = jnp.sum(weights, axis=-1, keepdims=True)
-        values = kv[:, :, pl.ds(HD, HD)].reshape(-1, HD)
-        summed = jnp.dot(weights.astype(jnp.bfloat16), values, preferred_element_type=jnp.float32)
-        ctx[rows, :] = summed / totals
+    nearest = z - 1 + 2 * (1 - (z + 3) // 4)
+    farthest = 3 * (1 - z // 2)
+    meets = (z, nearest, 6 - z - nearest - farthest, farthest)
+
+    def attend(k):
+        source = meets[k]
+        keys = kv[source, :, pl.ds(0, HD)]
+        values = kv[source, :, pl.ds(HD, HD)]
+        factor = math.log2(math.e) / math.sqrt(HD)
+        position = source * quad_rows + lax.broadcasted_iota(jnp.int32, (1, quad_rows), 1)
+        bias = jnp.where(position < limit_ref[0], 0.0, -1e30)
+        for i in range(query.shape[0] // BLOCK):
+            rows = pl.ds(i * BLOCK, BLOCK)
+            scores = lax.dot_general(
+                query[rows, :], keys, (((1,), (1,)), ((), ())), preferred_element_type=jnp.float32
+            ) + bias
+            peak = jnp.max(scores, axis=-1, keepdims=True)
+            if k > 0:
+                before = peaks[rows, :][:, :1]
+                peak = jnp.maximum(before, peak)
+                shrink = jnp.exp2((before - peak) * factor)
+            weights = jnp.exp2((scores - peak) * factor)
+            total = jnp.sum(weights, axis=-1, keepdims=True)
+            summed = jnp.dot(weights.astype(jnp.bfloat16), values, preferred_element_type=jnp.float32)
+            if k > 0:
+                total = total + totals[rows, :][:, :1] * shrink
+                summed = summed + ctx[rows, :] * shrink
+            if k < ZS - 1:
+                peaks[rows, :] = jnp.broadcast_to(peak, (BLOCK, HD))
+                totals[rows, :] = jnp.broadcast_to(total, (BLOCK, HD))
+                ctx[rows, :] = summed
+            else:
+                ctx[rows, :] = summed / total
 
     def share_context():
         ctx_out[...] = jnp.concatenate(
@@ -394,46 +443,53 @@
     own_feat.wait()
     features_to(0, p).start()
     features_to(1, p).start()
-    begin(OUT)
+    begin(PW1)
     for i, partner in enumerate(partners):
         columns_to(i, partner, p).wait_recv()
     spread(chain, 0)
+    begin(OUT)
+    begin(PW2)
     features_to(0, partners[0]).wait_recv()
     features_to(2, partners[0]).start()
-    begin(PW1)
     features_to(1, partners[1]).wait_recv()
     features_to(2, partners[2]).wait_recv()
     pl.when(z < ZS - 1)(lambda: edge(True).start())
     pl.when(z > 0)(lambda: edge(False).start())
     onward(chain, 0, 1)
-    pass_on(OUT, 1)
+    pass_on(PW1, 1)
     normalise()
     onward(chain, 0, 2)
-    pass_on(OUT, 2)
-    pass_on(PW1, 1)
+    pass_on(OUT, 1)
+    pass_on(PW2, 1)
+    cross(PW1, 1)
+    pass_on(PW1, 2)
     onward(chain, 0, 3)
     key_values()
     spread(chain, 1)
-    begin(PW2)
     queries()
+    cross(OUT, 1)
+    cross(PW2, 1)
+    pass_on(OUT, 2)
+    pass_on(PW2, 2)
+    cross(PW1, 2)
+    pass_on(PW1, 3)
+    attend(0)
+    onward(chain, 1, 1)
     pass_on(OUT, 3)
-    pass_on(PW1, 2)
-    onward(chain, 1, 1)
-    cross(OUT)
-    pass_on(PW1, 3)
-    pass_on(PW2, 1)
-    onward(chain, 1, 2)
-    swap(OUT)
-    pass_on(PW2, 2)
-    onward(chain, 1, 3)
-    attend(0)
-    cross(PW1)
     pass_on(PW2, 3)
     attend(1)
-    cross(PW2)
+    cross(PW1, 3)
+    cross(OUT, 2)
+    cross(PW2, 2)
+    onward(chain, 1, 2)
     attend(2)
+    cross(OUT, 3)
+    cross(PW2, 3)
+    onward(chain, 1, 3)
+    attend(3)
     share_context()
     swap(PW1)
+    swap(OUT)
     swap(PW2)
     arrive(OUT)
     collect_context()
@@ -490,6 +546,8 @@
             pltpu.VMEM((QUAD * local_rows, width), bf16),
             pltpu.VMEM((QUAD * local_rows + 2 * HALO, HD), bf16),
             pltpu.VMEM((QUAD * local_rows + 2 * HALO, HD), f32),
+            pltpu.VMEM((QUAD * local_rows + 2 * HALO, HD), f32),
+            pltpu.VMEM((QUAD * local_rows + 2 * HALO, HD), f32),
             pltpu.VMEM((QUAD * local_rows + 2 * HALO, HD), bf16),
             pltpu.VMEM((QUAD, wide, HD), bf16),
             pltpu.VMEM((wide, att), bf16),
@@ -501,7 +559,8 @@
             dma((COUNT + 1,)),
         ]
         + [dma((COUNT, ZS))] * 5
-        + [dma((COUNT,))] * 4
+        + [dma((COUNT, ZS, 2))] * 2
+        + [dma((COUNT, 2))] * 2
         + [dma((2, 3))] * 2
         + [dma((3,))] * 2
         + [dma((2,))] * 2

time: 99.9 us -> 67.1 us (0.67)
  Pallas kernels: 97.4 us -> 64.4 us
    pallas_call x1, Pallas kernels: 97.4 us -> 64.4 us  [per_device_kernel(): pl.pallas_call(block_kernel, out_shape=jax.ShapeDtypeStruct((local_rows,...]
where the time goes in v4:
time: 67.1 us; the launch traced here: 66.7 us
  Pallas kernels  64.4 us (96%)
  local copies, waits for them, and re-layouts  1.67 us (2%)
    pallas_call x1, Pallas kernels, per_device_kernel(): pl.pallas_call(block_kernel, out_shape=jax.ShapeDtypeStruct((local_rows,...  64.4 us
    unnamed x1, local copies, waits for them, and re-layouts  1.67 us

profile of v4, /device:TPU:0, one launch (start us, length us, event | category | flops | bytes accessed | tf_op | source)
XLA Modules:
  0.0 66.7 jit_solution(2465819140197174642)
XLA Ops:
  0.7 64.4 %shard_map.109 = bf16[128,1024]{1,0:T(8,128)(2,1)} custom-call(s32[1]{0:T(128)S(6)} %copy.13.limit_ref, bf16[128,1024]{1,0:T(8,128)(2,1)} %feat_ref.1, f32[1,1024]{1,0:T(1,128)} %bitcast.10, bf16[64,1536]{1,0:T(8,128)(2,1)} %qkv_ref.1, bf16[2,16,1024]{2,1,0:T(8,128)(2,1)} %bitcast.9, f32[1,1024]{1,0:T(1,128)} %bitcast.11, bf16[2,32,2048]{2,1,0:T(8,128)(2,1)} %bitcast.7, ...), custom_call_target="tpu_custom_call" | custom-call | tf_op jit(solution)/shard_map/pallas_call | solution.py:531
  65.0 1.7 %copy.14 = bf16[128,1024]{1,0:T(8,128)(2,1)} copy(bf16[128,1024]{1,0:T(8,128)(2,1)} %shard_map.109) | data formatting | bytes 524288

commit v5 on v4

--- a/solution.py
+++ b/solution.py
@@ -139,6 +139,7 @@
     gate, act,
     local_sem, zp_send, zm_send, z_recv, y_send, y_recv, x_send, x_recv, c_send, c_recv,
     peer_send, peer_recv, feat_send, feat_recv, edge_send, edge_recv, chain_p, chain_m, chain_recv,
+    half_send, half_recv,
 ):
     twin = lax.axis_index("groups")
     me = lax.axis_index("frames")
@@ -165,7 +166,7 @@
     for head in range(QUAD):
         for kind in range(3):
             stage[head, :, pl.ds(kind * HD, HD)] = qkv_ref[:, pl.ds((kind * QUAD + head) * HD, HD)]
-    g_qkv[z, p] = stage[p]
+    g_qkv[z, y, c] = stage[p]
     g_feat[0, pl.ds(local_rows - PAD, PAD), :] = jnp.zeros((PAD, width), jnp.bfloat16)
     g_feat[QUAD + 1, pl.ds(0, PAD), :] = jnp.zeros((PAD, width), jnp.bfloat16)
 
@@ -210,12 +211,16 @@
         return remote(part, part, c_send.at[q, half], c_recv.at[q, half], core)
 
     def chain(i, source, up):
-        part = (g_qkv, kv)[i].at[source]
+        part = kv.at[source] if i else g_qkv.at[source, twin]
         send = chain_p if up else chain_m
         return remote(part, part, send.at[i, source], chain_recv.at[i, source], above if up else below)
 
+    def columns_across(source, half):
+        part = g_qkv.at[source, half]
+        return remote(part, part, half_send.at[source], half_recv.at[source], other)
+
     def columns_to(i, sender, receiver):
-        return remote(stage.at[receiver], g_qkv.at[z, sender], peer_send.at[0, i], peer_recv.at[0, i], quad[i])
+        return remote(stage.at[receiver], g_qkv.at[z, sender // 2, sender % 2], peer_send.at[0, i], peer_recv.at[0, i], quad[i])
 
     def features_to(i, block):
         part = g_feat.at[block + 1]
@@ -268,7 +273,12 @@
     def begin(q):
         own[q].wait()
         spread(along_z, q)
+
+    def begin_across(q):
         own_along_y(q, y).start()
+
+    def columns_on(s):
+        onward(chain, 0, s, lambda source: columns_across(source, twin).start())
 
     def pass_on(q, s):
         def after(source):
@@ -330,11 +340,11 @@
         lax.fori_loop(0, QUAD, some, 0)
 
     def key_values():
-        weight = g_qkv[:, :, :, pl.ds(HD, 2 * HD)].reshape(-1, 2 * HD)
+        weight = g_qkv[:, :, :, :, pl.ds(HD, 2 * HD)].reshape(-1, 2 * HD)
         kv[z] = jnp.dot(rows_n[...], weight, preferred_element_type=jnp.float32).astype(jnp.bfloat16)
 
     def queries():
-        weight = g_qkv[:, :, :, pl.ds(0, HD)].reshape(-1, HD)
+        weight = g_qkv[:, :, :, :, pl.ds(0, HD)].reshape(-1, HD)
         query[pl.ds(0, quad_rows), :] = jnp.dot(
             rows_n[...], weight, preferred_element_type=jnp.float32
         ).astype(jnp.bfloat16)
@@ -407,7 +417,7 @@
             attended[:, pl.ds(at(j), CHUNK)] = ext[:, pl.ds(at(j), CHUNK)] + product
             return carry
 
-        lax.fori_loop(0, width // CHUNK, some, 0)
+        lax.fori_loop(0, width // CHUNK, some, 0, unroll=True)
         ext_n[...] = norm_rows(attended[...], ln2_ref[...])
 
     def convolve():
@@ -427,7 +437,7 @@
             act[:, cols] = (shifted / (1.0 + jnp.exp(-shifted))).astype(jnp.bfloat16)
             return carry
 
-        lax.fori_loop(0, width // CHUNK, some, 0)
+        lax.fori_loop(0, width // CHUNK, some, 0, unroll=True)
 
     def close():
         def some(j, carry):
@@ -436,7 +446,7 @@
             result_ref[:, cols] = (attended[pl.ds(HALO, local_rows), cols] + product).astype(jnp.bfloat16)
             return carry
 
-        lax.fori_loop(0, width // CHUNK, some, 0)
+        lax.fori_loop(0, width // CHUNK, some, 0, unroll=True)
 
     for i, partner in enumerate(partners):
         columns_to(i, p, partner).start()
@@ -451,44 +461,48 @@
     begin(PW2)
     features_to(0, partners[0]).wait_recv()
     features_to(2, partners[0]).start()
+    for q in (PW1, OUT, PW2):
+        begin_across(q)
+    columns_on(1)
     features_to(1, partners[1]).wait_recv()
     features_to(2, partners[2]).wait_recv()
     pl.when(z < ZS - 1)(lambda: edge(True).start())
     pl.when(z > 0)(lambda: edge(False).start())
-    onward(chain, 0, 1)
     pass_on(PW1, 1)
+    columns_on(2)
     normalise()
-    onward(chain, 0, 2)
+    columns_on(3)
     pass_on(OUT, 1)
     pass_on(PW2, 1)
-    cross(PW1, 1)
-    pass_on(PW1, 2)
-    onward(chain, 0, 3)
+    for s in range(1, ZS):
+        in_round(s, lambda source: columns_across(source, 1 - twin).wait_recv())
     key_values()
     spread(chain, 1)
     queries()
+    pass_on(PW1, 2)
+    cross(PW1, 1)
+    pass_on(OUT, 2)
+    pass_on(PW2, 2)
     cross(OUT, 1)
     cross(PW2, 1)
-    pass_on(OUT, 2)
-    pass_on(PW2, 2)
-    cross(PW1, 2)
-    pass_on(PW1, 3)
     attend(0)
     onward(chain, 1, 1)
+    pass_on(PW1, 3)
     pass_on(OUT, 3)
     pass_on(PW2, 3)
+    cross(PW1, 2)
     attend(1)
-    cross(PW1, 3)
+    onward(chain, 1, 2)
     cross(OUT, 2)
     cross(PW2, 2)
-    onward(chain, 1, 2)
+    cross(PW1, 3)
     attend(2)
     cross(OUT, 3)
     cross(PW2, 3)
     onward(chain, 1, 3)
+    swap(PW1)
     attend(3)
     share_context()
-    swap(PW1)
     swap(OUT)
     swap(PW2)
     arrive(OUT)
@@ -503,6 +517,8 @@
         finish(q)
     for i in range(2):
         sent(chain, i)
+    for s in range(1, ZS):
+        in_round(s, lambda source: columns_across(source, twin).wait_send())
     for i, partner in enumerate(partners):
         columns_to(i, p, partner).wait_send()
         context_to(i, p, partner).wait_send()
@@ -537,7 +553,7 @@
         out_specs=vmem,
         scratch_shapes=[
             pltpu.VMEM((QUAD, w_qkv.shape[0], 3 * HD), bf16),
-            pltpu.VMEM((ZS, QUAD, w_qkv.shape[0], 3 * HD), bf16),
+            pltpu.VMEM((ZS, 2, 2, w_qkv.shape[0], 3 * HD), bf16),
             pltpu.VMEM((QUAD + 2, local_rows, width), bf16),
             pltpu.VMEM((ZS, QUAD * local_rows, 2 * HD), bf16),
             pltpu.VMEM(grid + shards[0].shape, bf16),
@@ -564,7 +580,8 @@
         + [dma((2, 3))] * 2
         + [dma((3,))] * 2
         + [dma((2,))] * 2
-        + [dma((2, ZS))] * 3,
+        + [dma((2, ZS))] * 3
+        + [dma((ZS,))] * 2,
         compiler_params=pltpu.CompilerParams(
             collective_id=0, has_side_effects=True, vmem_limit_bytes=56 * 1024 * 1024
         ),

time: 67.1 us -> 65.4 us (0.975)
  Pallas kernels: 64.4 us -> 62.9 us
    pallas_call x1, Pallas kernels: 64.4 us -> 62.9 us  [per_device_kernel(): pl.pallas_call(block_kernel, out_shape=jax.ShapeDtypeStruct((local_rows,...]
where the time goes in v5:
time: 65.4 us; the launch traced here: 65.2 us
  Pallas kernels  62.9 us (96%)
  local copies, waits for them, and re-layouts  1.67 us (3%)
  between operations  0.66 us (1%)
    pallas_call x1, Pallas kernels, per_device_kernel(): pl.pallas_call(block_kernel, out_shape=jax.ShapeDtypeStruct((local_rows,...  62.9 us
    unnamed x1, local copies, waits for them, and re-layouts  1.67 us

profile of v5, /device:TPU:0, one launch (start us, length us, event | category | flops | bytes accessed | tf_op | source)
XLA Modules:
  0.0 65.2 jit_solution(13085118068285517155)
XLA Ops:
  0.7 62.9 %shard_map.109 = bf16[128,1024]{1,0:T(8,128)(2,1)} custom-call(s32[1]{0:T(128)S(6)} %copy.13.limit_ref, bf16[128,1024]{1,0:T(8,128)(2,1)} %feat_ref.1, f32[1,1024]{1,0:T(1,128)} %bitcast.10, bf16[64,1536]{1,0:T(8,128)(2,1)} %qkv_ref.1, bf16[2,16,1024]{2,1,0:T(8,128)(2,1)} %bitcast.9, f32[1,1024]{1,0:T(1,128)} %bitcast.11, bf16[2,32,2048]{2,1,0:T(8,128)(2,1)} %bitcast.7, ...), custom_call_target="tpu_custom_call" | custom-call | tf_op jit(solution)/shard_map/pallas_call | solution.py:547
  63.5 1.7 %copy.14 = bf16[128,1024]{1,0:T(8,128)(2,1)} copy(bf16[128,1024]{1,0:T(8,128)(2,1)} %shard_map.109) | data formatting | bytes 524288

commit v6 on v5

--- a/solution.py
+++ b/solution.py
@@ -464,68 +464,69 @@
     for q in (PW1, OUT, PW2):
         begin_across(q)
     columns_on(1)
+    pass_on(PW1, 1)
+    pass_on(OUT, 1)
+    pass_on(PW2, 1)
+    columns_on(2)
     features_to(1, partners[1]).wait_recv()
     features_to(2, partners[2]).wait_recv()
     pl.when(z < ZS - 1)(lambda: edge(True).start())
     pl.when(z > 0)(lambda: edge(False).start())
-    pass_on(PW1, 1)
-    columns_on(2)
+    pass_on(PW1, 2)
+    pass_on(OUT, 2)
     normalise()
+    pass_on(PW2, 2)
     columns_on(3)
-    pass_on(OUT, 1)
-    pass_on(PW2, 1)
     for s in range(1, ZS):
         in_round(s, lambda source: columns_across(source, 1 - twin).wait_recv())
     key_values()
     spread(chain, 1)
-    queries()
-    pass_on(PW1, 2)
-    cross(PW1, 1)
-    pass_on(OUT, 2)
-    pass_on(PW2, 2)
-    cross(OUT, 1)
-    cross(PW2, 1)
-    attend(0)
-    onward(chain, 1, 1)
     pass_on(PW1, 3)
     pass_on(OUT, 3)
     pass_on(PW2, 3)
+    cross(PW1, 1)
+    cross(OUT, 1)
+    queries()
+    cross(PW2, 1)
     cross(PW1, 2)
+    cross(OUT, 2)
+    cross(PW2, 2)
+    attend(0)
+    onward(chain, 1, 1)
+    cross(PW1, 3)
+    cross(OUT, 3)
+    cross(PW2, 3)
     attend(1)
     onward(chain, 1, 2)
-    cross(OUT, 2)
-    cross(PW2, 2)
-    cross(PW1, 3)
     attend(2)
-    cross(OUT, 3)
-    cross(PW2, 3)
+    swap(OUT)
+    swap(PW1)
+    swap(PW2)
     onward(chain, 1, 3)
-    swap(PW1)
     attend(3)
     share_context()
-    swap(OUT)
-    swap(PW2)
-    arrive(OUT)
-    collect_context()
-    project()
-    arrive(PW1)
-    convolve()
-    arrive(PW2)
-    close()
-
-    for q in range(COUNT):
-        finish(q)
-    for i in range(2):
-        sent(chain, i)
-    for s in range(1, ZS):
-        in_round(s, lambda source: columns_across(source, twin).wait_send())
     for i, partner in enumerate(partners):
         columns_to(i, p, partner).wait_send()
-        context_to(i, p, partner).wait_send()
     for i, block in enumerate((p, p, partners[0])):
         features_to(i, block).wait_send()
     pl.when(z < ZS - 1)(lambda: edge(True).wait_send())
     pl.when(z > 0)(lambda: edge(False).wait_send())
+    for s in range(1, ZS):
+        in_round(s, lambda source: columns_across(source, twin).wait_send())
+    sent(chain, 0)
+    arrive(OUT)
+    collect_context()
+    project()
+    finish(OUT)
+    arrive(PW1)
+    convolve()
+    finish(PW1)
+    arrive(PW2)
+    close()
+    finish(PW2)
+    sent(chain, 1)
+    for i, partner in enumerate(partners):
+        context_to(i, p, partner).wait_send()
 
 
 def per_device_kernel(

time: 65.4 us -> 64.5 us (0.986)
  Pallas kernels: 62.9 us -> 62 us
    pallas_call x1, Pallas kernels: 62.9 us -> 62 us  [per_device_kernel(): pl.pallas_call(block_kernel, out_shape=jax.ShapeDtypeStruct((local_rows,...]
where the time goes in v6:
time: 64.5 us; the launch traced here: 64.3 us
  Pallas kernels  62 us (96%)
  local copies, waits for them, and re-layouts  1.67 us (3%)
  between operations  0.66 us (1%)
    pallas_call x1, Pallas kernels, per_device_kernel(): pl.pallas_call(block_kernel, out_shape=jax.ShapeDtypeStruct((local_rows,...  62 us
    unnamed x1, local copies, waits for them, and re-layouts  1.67 us

profile of v6, /device:TPU:0, one launch (start us, length us, event | category | flops | bytes accessed | tf_op | source)
XLA Modules:
  0.0 64.3 jit_solution(17232335048812073593)
XLA Ops:
  0.7 62.0 %shard_map.109 = bf16[128,1024]{1,0:T(8,128)(2,1)} custom-call(s32[1]{0:T(128)S(6)} %copy.13.limit_ref, bf16[128,1024]{1,0:T(8,128)(2,1)} %feat_ref.1, f32[1,1024]{1,0:T(1,128)} %bitcast.10, bf16[64,1536]{1,0:T(8,128)(2,1)} %qkv_ref.1, bf16[2,16,1024]{2,1,0:T(8,128)(2,1)} %bitcast.9, f32[1,1024]{1,0:T(1,128)} %bitcast.11, bf16[2,32,2048]{2,1,0:T(8,128)(2,1)} %bitcast.7, ...), custom_call_target="tpu_custom_call" | custom-call | tf_op jit(solution)/shard_map/pallas_call | solution.py:548
  62.7 1.7 %copy.14 = bf16[128,1024]{1,0:T(8,128)(2,1)} copy(bf16[128,1024]{1,0:T(8,128)(2,1)} %shard_map.109) | data formatting | bytes 524288

commit v7 on v6

--- a/solution.py
+++ b/solution.py
@@ -458,53 +458,61 @@
         columns_to(i, partner, p).wait_recv()
     spread(chain, 0)
     begin(OUT)
-    begin(PW2)
     features_to(0, partners[0]).wait_recv()
     features_to(2, partners[0]).start()
-    for q in (PW1, OUT, PW2):
-        begin_across(q)
+    begin_across(PW1)
+    begin_across(OUT)
     columns_on(1)
     pass_on(PW1, 1)
-    pass_on(OUT, 1)
-    pass_on(PW2, 1)
-    columns_on(2)
     features_to(1, partners[1]).wait_recv()
     features_to(2, partners[2]).wait_recv()
     pl.when(z < ZS - 1)(lambda: edge(True).start())
     pl.when(z > 0)(lambda: edge(False).start())
+    columns_on(2)
+    pass_on(OUT, 1)
+    normalise()
+    columns_on(3)
     pass_on(PW1, 2)
     pass_on(OUT, 2)
-    normalise()
-    pass_on(PW2, 2)
-    columns_on(3)
     for s in range(1, ZS):
         in_round(s, lambda source: columns_across(source, 1 - twin).wait_recv())
     key_values()
     spread(chain, 1)
+    cross(PW1, 1)
     pass_on(PW1, 3)
     pass_on(OUT, 3)
-    pass_on(PW2, 3)
-    cross(PW1, 1)
     cross(OUT, 1)
     queries()
-    cross(PW2, 1)
     cross(PW1, 2)
     cross(OUT, 2)
-    cross(PW2, 2)
     attend(0)
     onward(chain, 1, 1)
+    begin(PW2)
+    begin_across(PW2)
     cross(PW1, 3)
     cross(OUT, 3)
-    cross(PW2, 3)
     attend(1)
     onward(chain, 1, 2)
+    pass_on(PW2, 1)
     attend(2)
     swap(OUT)
     swap(PW1)
-    swap(PW2)
     onward(chain, 1, 3)
+    pass_on(PW2, 2)
+    cross(PW2, 1)
     attend(3)
     share_context()
+    pass_on(PW2, 3)
+    cross(PW2, 2)
+    arrive(OUT)
+    collect_context()
+    cross(PW2, 3)
+    project()
+    swap(PW2)
+    finish(OUT)
+    arrive(PW1)
+    convolve()
+    finish(PW1)
     for i, partner in enumerate(partners):
         columns_to(i, p, partner).wait_send()
     for i, block in enumerate((p, p, partners[0])):
@@ -514,13 +522,6 @@
     for s in range(1, ZS):
         in_round(s, lambda source: columns_across(source, twin).wait_send())
     sent(chain, 0)
-    arrive(OUT)
-    collect_context()
-    project()
-    finish(OUT)
-    arrive(PW1)
-    convolve()
-    finish(PW1)
     arrive(PW2)
     close()
     finish(PW2)

time: 64.5 us -> 65.3 us (1.012)
  Pallas kernels: 62 us -> 62.8 us
    pallas_call x1, Pallas kernels: 62 us -> 62.8 us  [per_device_kernel(): pl.pallas_call(block_kernel, out_shape=jax.ShapeDtypeStruct((local_rows,...]
where the time goes in v7:
time: 65.3 us; the launch traced here: 65.1 us
  Pallas kernels  62.8 us (96%)
  local copies, waits for them, and re-layouts  1.67 us (3%)
  between operations  0.66 us (1%)
    pallas_call x1, Pallas kernels, per_device_kernel(): pl.pallas_call(block_kernel, out_shape=jax.ShapeDtypeStruct((local_rows,...  62.8 us
    unnamed x1, local copies, waits for them, and re-layouts  1.67 us

profile of v7, /device:TPU:0, one launch (start us, length us, event | category | flops | bytes accessed | tf_op | source)
XLA Modules:
  0.0 65.1 jit_solution(12522999274463877566)
XLA Ops:
  0.7 62.8 %shard_map.109 = bf16[128,1024]{1,0:T(8,128)(2,1)} custom-call(s32[1]{0:T(128)S(6)} %copy.13.limit_ref, bf16[128,1024]{1,0:T(8,128)(2,1)} %feat_ref.1, f32[1,1024]{1,0:T(1,128)} %bitcast.10, bf16[64,1536]{1,0:T(8,128)(2,1)} %qkv_ref.1, bf16[2,16,1024]{2,1,0:T(8,128)(2,1)} %bitcast.9, f32[1,1024]{1,0:T(1,128)} %bitcast.11, bf16[2,32,2048]{2,1,0:T(8,128)(2,1)} %bitcast.7, ...), custom_call_target="tpu_custom_call" | custom-call | tf_op jit(solution)/shard_map/pallas_call | solution.py:549
  63.4 1.7 %copy.14 = bf16[128,1024]{1,0:T(8,128)(2,1)} copy(bf16[128,1024]{1,0:T(8,128)(2,1)} %shard_map.109) | data formatting | bytes 524288

commit v8 on v6

--- a/solution.py
+++ b/solution.py
@@ -120,8 +120,8 @@
 PAD = 16
 HALO = 8
 BLOCK = 176
-OUT, PW1, PW2 = range(3)
-COUNT = 3
+REST = 0
+COUNT = 1
 
 
 def norm_rows(values, gain):
@@ -135,7 +135,7 @@
 def block_kernel(
     limit_ref, feat_ref, ln1_ref, qkv_ref, out_w_ref, ln2_ref, pw1_ref, dw_ref, bns_ref, bnb_ref, pw2_ref,
     result_ref,
-    stage, g_qkv, g_feat, kv, g_out, g_pw1, g_pw2, rows_n, query, ctx, peaks, totals, ctx_out, g_ctx, context, ext, ext_n, attended,
+    stage, g_qkv, g_feat, kv, g_rest, rows_n, query, ctx, peaks, totals, ctx_out, g_ctx, context, ext, ext_n, attended,
     gate, act,
     local_sem, zp_send, zm_send, z_recv, y_send, y_recv, x_send, x_recv, c_send, c_recv,
     peer_send, peer_recv, feat_send, feat_recv, edge_send, edge_recv, chain_p, chain_m, chain_recv,
@@ -148,19 +148,27 @@
     width = ext.shape[1]
     local_rows = feat_ref.shape[0]
     quad_rows = QUAD * local_rows
-    gathered = (g_out, g_pw1, g_pw2)
-    shards = (out_w_ref, pw1_ref, pw2_ref)
+    gathered = (g_rest,)
     above, below = {"frames": me + 4}, {"frames": me - 4}
     partners = (QUAD // 2 * (1 - y) + c, 2 * y + 1 - c, QUAD // 2 * (1 - y) + 1 - c)
     quad = [{"frames": z * QUAD + partner} for partner in partners]
     across, core = quad[0], quad[1]
     other = {"groups": 1 - twin}
 
-    own = [
-        pltpu.make_async_copy(shards[q], gathered[q].at[z, y, c], local_sem.at[q])
-        for q in range(COUNT)
-    ]
-    own_feat = pltpu.make_async_copy(feat_ref, g_feat.at[p + 1], local_sem.at[COUNT])
+    counts = (out_w_ref.shape[1], pw1_ref.shape[1], pw1_ref.shape[1], pw2_ref.shape[1])
+    starts = [sum(counts[:i]) for i in range(4)]
+    own = []
+    for half in range(2):
+        pieces = (
+            out_w_ref.at[half],
+            pw1_ref.at[half, :, pl.ds(0, width)],
+            pw1_ref.at[half, :, pl.ds(width, width)],
+            pw2_ref.at[half],
+        )
+        for i in range(4):
+            part = g_rest.at[z, y, c, half, pl.ds(starts[i], counts[i])]
+            own.append(pltpu.make_async_copy(pieces[i], part, local_sem.at[4 * half + i]))
+    own_feat = pltpu.make_async_copy(feat_ref, g_feat.at[p + 1], local_sem.at[8])
     for copy in own + [own_feat]:
         copy.start()
     for head in range(QUAD):
@@ -271,7 +279,8 @@
         pl.when(z + s <= ZS - 1)(lambda: do(z + s))
 
     def begin(q):
-        own[q].wait()
+        for copy in own:
+            copy.wait()
         spread(along_z, q)
 
     def begin_across(q):
@@ -323,8 +332,8 @@
         for half in range(2):
             to_core(q, c, half).wait_send()
 
-    def columns(ref, start):
-        block = ref[:, :, :, :, :, pl.ds(start, CHUNK)]
+    def columns(i, start):
+        block = g_rest[:, :, :, :, pl.ds(starts[i], counts[i]), pl.ds(start, CHUNK)]
         return block.reshape(-1, CHUNK)
 
     def at(j):
@@ -369,7 +378,7 @@
     def attend(k):
         source = meets[k]
         keys = kv[source, :, pl.ds(0, HD)]
-        values = kv[source, :, pl.ds(HD, HD)]
+        values = jnp.concatenate([kv[source, :, pl.ds(HD, HD)], jnp.ones((quad_rows, HD), jnp.bfloat16)], axis=1)
         factor = math.log2(math.e) / math.sqrt(HD)
         position = source * quad_rows + lax.broadcasted_iota(jnp.int32, (1, quad_rows), 1)
         bias = jnp.where(position < limit_ref[0], 0.0, -1e30)
@@ -384,14 +393,14 @@
                 peak = jnp.maximum(before, peak)
                 shrink = jnp.exp2((before - peak) * factor)
             weights = jnp.exp2((scores - peak) * factor)
-            total = jnp.sum(weights, axis=-1, keepdims=True)
             summed = jnp.dot(weights.astype(jnp.bfloat16), values, preferred_element_type=jnp.float32)
+            summed, total = summed[:, :HD], summed[:, HD:]
             if k > 0:
-                total = total + totals[rows, :][:, :1] * shrink
+                total = total + totals[rows, :] * shrink
                 summed = summed + ctx[rows, :] * shrink
             if k < ZS - 1:
                 peaks[rows, :] = jnp.broadcast_to(peak, (BLOCK, HD))
-                totals[rows, :] = jnp.broadcast_to(total, (BLOCK, HD))
+                totals[rows, :] = total
                 ctx[rows, :] = summed
             else:
                 ctx[rows, :] = summed / total
@@ -413,7 +422,7 @@
 
     def project():
         def some(j, carry):
-            product = jnp.dot(context[...], columns(g_out, at(j)), preferred_element_type=jnp.float32)
+            product = jnp.dot(context[...], columns(0, at(j)), preferred_element_type=jnp.float32)
             attended[:, pl.ds(at(j), CHUNK)] = ext[:, pl.ds(at(j), CHUNK)] + product
             return carry
 
@@ -422,8 +431,8 @@
 
     def convolve():
         def some(j, carry):
-            value = jnp.dot(ext_n[...], columns(g_pw1, at(j)), preferred_element_type=jnp.float32)
-            gates = jnp.dot(ext_n[...], columns(g_pw1, at(j) + width), preferred_element_type=jnp.float32)
+            value = jnp.dot(ext_n[...], columns(1, at(j)), preferred_element_type=jnp.float32)
+            gates = jnp.dot(ext_n[...], columns(2, at(j)), preferred_element_type=jnp.float32)
             frame = me * local_rows - HALO + lax.broadcasted_iota(jnp.int32, value.shape, 0)
             valid = (frame >= 0) & (frame < limit_ref[0])
             gated = jnp.where(valid, value * jax.nn.sigmoid(gates), 0.0)
@@ -442,7 +451,7 @@
     def close():
         def some(j, carry):
             cols = pl.ds(at(j), CHUNK)
-            product = jnp.dot(act[...], columns(g_pw2, at(j)), preferred_element_type=jnp.float32)
+            product = jnp.dot(act[...], columns(3, at(j)), preferred_element_type=jnp.float32)
             result_ref[:, cols] = (attended[pl.ds(HALO, local_rows), cols] + product).astype(jnp.bfloat16)
             return carry
 
@@ -453,55 +462,38 @@
     own_feat.wait()
     features_to(0, p).start()
     features_to(1, p).start()
-    begin(PW1)
+    begin(REST)
     for i, partner in enumerate(partners):
         columns_to(i, partner, p).wait_recv()
     spread(chain, 0)
-    begin(OUT)
-    begin(PW2)
     features_to(0, partners[0]).wait_recv()
     features_to(2, partners[0]).start()
-    for q in (PW1, OUT, PW2):
-        begin_across(q)
+    begin_across(REST)
     columns_on(1)
-    pass_on(PW1, 1)
-    pass_on(OUT, 1)
-    pass_on(PW2, 1)
-    columns_on(2)
+    pass_on(REST, 1)
     features_to(1, partners[1]).wait_recv()
     features_to(2, partners[2]).wait_recv()
     pl.when(z < ZS - 1)(lambda: edge(True).start())
     pl.when(z > 0)(lambda: edge(False).start())
-    pass_on(PW1, 2)
-    pass_on(OUT, 2)
+    columns_on(2)
     normalise()
-    pass_on(PW2, 2)
     columns_on(3)
+    pass_on(REST, 2)
     for s in range(1, ZS):
         in_round(s, lambda source: columns_across(source, 1 - twin).wait_recv())
     key_values()
     spread(chain, 1)
-    pass_on(PW1, 3)
-    pass_on(OUT, 3)
-    pass_on(PW2, 3)
-    cross(PW1, 1)
-    cross(OUT, 1)
+    cross(REST, 1)
     queries()
-    cross(PW2, 1)
-    cross(PW1, 2)
-    cross(OUT, 2)
-    cross(PW2, 2)
     attend(0)
+    pass_on(REST, 3)
+    cross(REST, 2)
     onward(chain, 1, 1)
-    cross(PW1, 3)
-    cross(OUT, 3)
-    cross(PW2, 3)
     attend(1)
+    cross(REST, 3)
     onward(chain, 1, 2)
     attend(2)
-    swap(OUT)
-    swap(PW1)
-    swap(PW2)
+    swap(REST)
     onward(chain, 1, 3)
     attend(3)
     share_context()
@@ -514,16 +506,12 @@
     for s in range(1, ZS):
         in_round(s, lambda source: columns_across(source, twin).wait_send())
     sent(chain, 0)
-    arrive(OUT)
+    arrive(REST)
     collect_context()
     project()
-    finish(OUT)
-    arrive(PW1)
     convolve()
-    finish(PW1)
-    arrive(PW2)
     close()
-    finish(PW2)
+    finish(REST)
     sent(chain, 1)
     for i, partner in enumerate(partners):
         context_to(i, p, partner).wait_send()
@@ -557,9 +545,7 @@
             pltpu.VMEM((ZS, 2, 2, w_qkv.shape[0], 3 * HD), bf16),
             pltpu.VMEM((QUAD + 2, local_rows, width), bf16),
             pltpu.VMEM((ZS, QUAD * local_rows, 2 * HD), bf16),
-            pltpu.VMEM(grid + shards[0].shape, bf16),
-            pltpu.VMEM(grid + shards[1].shape, bf16),
-            pltpu.VMEM(grid + shards[2].shape, bf16),
+            pltpu.VMEM(grid + (2, sum(w.shape[1] for w in shards) + shards[1].shape[1], width), bf16),
             pltpu.VMEM((QUAD * local_rows, width), bf16),
             pltpu.VMEM((QUAD * local_rows + 2 * HALO, HD), bf16),
             pltpu.VMEM((QUAD * local_rows + 2 * HALO, HD), f32),
@@ -573,7 +559,7 @@
             pltpu.VMEM((wide, width), f32),
             pltpu.VMEM((wide, CHUNK), f32),
             pltpu.VMEM((local_rows, width), bf16),
-            dma((COUNT + 1,)),
+            dma((9,)),
         ]
         + [dma((COUNT, ZS))] * 5
         + [dma((COUNT, ZS, 2))] * 2

time: 64.5 us -> 64.6 us (level)
  no operation moved by 1% of the time
where the time goes in v8:
time: 64.6 us; the launch traced here: 64.4 us
  Pallas kernels  62.1 us (96%)
  local copies, waits for them, and re-layouts  1.67 us (3%)
  between operations  0.66 us (1%)
    pallas_call x1, Pallas kernels, per_device_kernel(): pl.pallas_call(block_kernel, out_shape=jax.ShapeDtypeStruct((local_rows,...  62.1 us
    unnamed x1, local copies, waits for them, and re-layouts  1.67 us

profile of v8, /device:TPU:0, one launch (start us, length us, event | category | flops | bytes accessed | tf_op | source)
XLA Modules:
  0.0 64.4 jit_solution(5679301393700304185)
XLA Ops:
  0.7 62.1 %shard_map.109 = bf16[128,1024]{1,0:T(8,128)(2,1)} custom-call(s32[1]{0:T(128)S(6)} %copy.13.limit_ref, bf16[128,1024]{1,0:T(8,128)(2,1)} %feat_ref.1, f32[1,1024]{1,0:T(1,128)} %bitcast.10, bf16[64,1536]{1,0:T(8,128)(2,1)} %qkv_ref.1, bf16[2,16,1024]{2,1,0:T(8,128)(2,1)} %bitcast.9, f32[1,1024]{1,0:T(1,128)} %bitcast.11, bf16[2,32,2048]{2,1,0:T(8,128)(2,1)} %bitcast.7, ...), custom_call_target="tpu_custom_call" | custom-call | tf_op jit(solution)/shard_map/pallas_call | solution.py:536
  62.7 1.7 %copy.14 = bf16[128,1024]{1,0:T(8,128)(2,1)} copy(bf16[128,1024]{1,0:T(8,128)(2,1)} %shard_map.109) | data formatting | bytes 524288

commit v9 on v8

--- a/solution.py
+++ b/solution.py
@@ -470,28 +470,28 @@
     features_to(2, partners[0]).start()
     begin_across(REST)
     columns_on(1)
-    pass_on(REST, 1)
     features_to(1, partners[1]).wait_recv()
     features_to(2, partners[2]).wait_recv()
     pl.when(z < ZS - 1)(lambda: edge(True).start())
     pl.when(z > 0)(lambda: edge(False).start())
     columns_on(2)
+    pass_on(REST, 1)
     normalise()
     columns_on(3)
-    pass_on(REST, 2)
     for s in range(1, ZS):
         in_round(s, lambda source: columns_across(source, 1 - twin).wait_recv())
     key_values()
     spread(chain, 1)
+    pass_on(REST, 2)
     cross(REST, 1)
     queries()
+    onward(chain, 1, 1)
     attend(0)
     pass_on(REST, 3)
     cross(REST, 2)
-    onward(chain, 1, 1)
+    onward(chain, 1, 2)
     attend(1)
     cross(REST, 3)
-    onward(chain, 1, 2)
     attend(2)
     swap(REST)
     onward(chain, 1, 3)
@@ -510,9 +510,9 @@
     collect_context()
     project()
     convolve()
-    close()
     finish(REST)
     sent(chain, 1)
+    close()
     for i, partner in enumerate(partners):
         context_to(i, p, partner).wait_send()
 

time: 64.6 us -> 64.5 us (level)
  no operation moved by 1% of the time
where the time goes in v9:
time: 64.5 us; the launch traced here: 64.3 us
  Pallas kernels  61.9 us (96%)
  local copies, waits for them, and re-layouts  1.67 us (3%)
  between operations  0.66 us (1%)
    pallas_call x1, Pallas kernels, per_device_kernel(): pl.pallas_call(block_kernel, out_shape=jax.ShapeDtypeStruct((local_rows,...  61.9 us
    unnamed x1, local copies, waits for them, and re-layouts  1.67 us

profile of v9, /device:TPU:0, one launch (start us, length us, event | category | flops | bytes accessed | tf_op | source)
XLA Modules:
  0.0 64.3 jit_solution(15838004513784228855)
XLA Ops:
  0.7 61.9 %shard_map.109 = bf16[128,1024]{1,0:T(8,128)(2,1)} custom-call(s32[1]{0:T(128)S(6)} %copy.13.limit_ref, bf16[128,1024]{1,0:T(8,128)(2,1)} %feat_ref.1, f32[1,1024]{1,0:T(1,128)} %bitcast.10, bf16[64,1536]{1,0:T(8,128)(2,1)} %qkv_ref.1, bf16[2,16,1024]{2,1,0:T(8,128)(2,1)} %bitcast.9, f32[1,1024]{1,0:T(1,128)} %bitcast.11, bf16[2,32,2048]{2,1,0:T(8,128)(2,1)} %bitcast.7, ...), custom_call_target="tpu_custom_call" | custom-call | tf_op jit(solution)/shard_map/pallas_call | solution.py:536
  62.6 1.7 %copy.14 = bf16[128,1024]{1,0:T(8,128)(2,1)} copy(bf16[128,1024]{1,0:T(8,128)(2,1)} %shard_map.109) | data formatting | bytes 524288
